TPU v7x, 32 devices: a whole 2x2x4 slice. The times are simulated.
32 devices in a mesh: mem: 4 (over z), lat: 2 (over x), lon: 4 (over y, core).
Axes of the slice: x: 2, y: 2, z: 4, core: 2. Of those that a mesh axis runs over, the one named last changes fastest.
Arguments:
- gradient: float32 [4, 64, 1024], P('mem', 'lat', 'lon'), may hold values from -6 to 6
- perturbations: bfloat16 [20, 4, 64, 1024], P('mem', None, 'lat', 'lon'), may hold values from -6 to 6
- filter_coef: float32 [5, 64, 1024], P(None, 'lat', 'lon'), may hold values from 0.1 to 0.6
Outputs:
- hess_grad: float32 [4, 64, 1024], P('mem', 'lat', 'lon')
All inputs are finite; a program needn't handle non-finite values.
Results may differ from a plain program's by a relative error of at most 0.0003.
Values may be sent and summed in bfloat16 or wider, within the bound.
A program may use at most 64 MiB of HBM per device.

v0:
```python
import jax
import jax.numpy as jnp
from jax import lax
from jax.sharding import PartitionSpec as P


def extended(block, sides, width):
    for axis, dim in sides:
        count = lax.axis_size(axis)
        forward = [(i, i + 1) for i in range(count - 1)]
        backward = [(target, source) for source, target in forward]
        low = lax.ppermute(
            lax.slice_in_dim(block, block.shape[dim] - width, None, axis=dim), axis, forward
        )
        high = lax.ppermute(lax.slice_in_dim(block, 0, width, axis=dim), axis, backward)
        block = jnp.concatenate([low, block, high], axis=dim)
    return block


def trim_margin(stencil, margin, target):
    extra = margin - target
    return stencil[..., extra : stencil.shape[-2] - extra, extra : stencil.shape[-1] - extra]


def forward_pass(values, stencil, stencil_margin, margin):
    coefs = trim_margin(stencil, stencil_margin, margin - 1)
    out = coefs[0] * values[..., 1:-1, 1:-1] + coefs[1] * values[..., :-2, 1:-1]
    out = out + coefs[2] * values[..., 2:, 1:-1]
    out = out + coefs[3] * values[..., 1:-1, :-2]
    return out + coefs[4] * values[..., 1:-1, 2:]


def adjoint_pass(values, stencil, stencil_margin, margin):
    coefs = trim_margin(stencil, stencil_margin, margin)
    north_term = coefs[1] * values
    south_term = coefs[2] * values
    west_term = coefs[3] * values
    east_term = coefs[4] * values
    out = coefs[0][1:-1, 1:-1] * values[..., 1:-1, 1:-1] + north_term[..., 2:, 1:-1]
    out = out + south_term[..., :-2, 1:-1] + west_term[..., 1:-1, 2:]
    return out + east_term[..., 1:-1, :-2]


def inside_mask(margin, row_count, col_count):
    row_index = (
        lax.axis_index("lat") * row_count
        - margin
        + jnp.arange(row_count + 2 * margin, dtype=jnp.int32)
    )
    col_index = (
        lax.axis_index("lon") * col_count
        - margin
        + jnp.arange(col_count + 2 * margin, dtype=jnp.int32)
    )
    row_inside = (row_index >= 0) & (row_index < row_count * lax.axis_size("lat"))
    col_inside = (col_index >= 0) & (col_index < col_count * lax.axis_size("lon"))
    return (row_inside[:, None] & col_inside[None, :]).astype(jnp.float32)


def deep_passes(padded, stencil, row_count, col_count):
    padded = adjoint_pass(padded, stencil, 4, 4) * inside_mask(3, row_count, col_count)
    padded = adjoint_pass(padded, stencil, 4, 3) * inside_mask(2, row_count, col_count)
    padded = forward_pass(padded, stencil, 4, 2) * inside_mask(1, row_count, col_count)
    return forward_pass(padded, stencil, 4, 1)


def apply_filter(values, filter_coef):
    row_count = filter_coef.shape[1]
    col_count = filter_coef.shape[2]
    stencil = extended(filter_coef, (("lat", 1), ("lon", 2)), 4)
    padded = extended(values, (("lat", 2), ("lon", 3)), 4)
    return deep_passes(padded, stencil, row_count, col_count)


def body(gradient, perturbations, filter_coef):
    member_vals = perturbations.astype(jnp.float32)
    gathered = lax.all_gather(gradient, "mem", axis=0, tiled=True)
    filtered = apply_filter(member_vals * gathered[None], filter_coef)
    summed = jnp.sum(member_vals * filtered, axis=0)
    reduced = lax.psum_scatter(summed, "mem", scatter_dimension=0, tiled=True)
    member_count = perturbations.shape[0] * lax.axis_size("mem")
    return reduced * (1.0 / (member_count - 1))


def solution(mesh):
    return jax.shard_map(
        body,
        mesh=mesh,
        in_specs=(P("mem", "lat", "lon"), P("mem", None, "lat", "lon"), P(None, "lat", "lon")),
        out_specs=P("mem", "lat", "lon"),
        check_vma=False,
    )
```

profile of v0, /device:TPU:0, one launch (start us, length us, event | category | flops | bytes accessed | tf_op | source)
XLA Modules:
  0.0 92.3 jit_solution(9748322898297690824)
XLA Ops:
  6.5 15.4 %all_gather.3 = f32[4,32,256]{2,1,0:T(8,128)S(1)} all-gather(f32[1,32,256]{2,1,0:T(8,128)} %param.3), channel_id=1, replica_groups=mesh['mem'=4,'lat'=2,'lon'=4] {'mem'}, dimensions={0}, use_global_device_ids=true | all-gather | bytes 163840 | tf_op jit(solution)/shard_map/all_gather | solution.py:77
  21.9 1.0 %convert_multiply_fusion.1 = f32[5,4,32,256]{3,2,1,0:T(8,128)S(1)} fusion(bf16[5,4,32,256]{3,2,1,0:T(8,128)(2,1)} %param.4, f32[4,32,256]{2,1,0:T(8,128)S(1)} %all_gather.3), kind=kLoop, calls=%fused_computation.33 | loop fusion | flops 327680 | bytes 1114112 | tf_op jit(solution)/shard_map/mul | solution.py:78
  23.0 3.4 %collective-permute-start.4 = (f32[5,4,4,256]{3,2,1,0:T(4,128)S(1)}, f32[5,4,4,256]{3,2,1,0:T(4,128)S(1)}, u32[]{:S(2)}, u32[]{:S(2)}) collective-permute-start(f32[5,4,4,256]{3,2,1,0:T(4,128)S(1)} %get-tuple-element.7), channel_id=1, source_target_pairs={{0,4},{1,5},{2,6},{3,7},{8,12},{9,13},{10,14},{11,15},{16,20},{17,... | collective-permute-start | bytes 245768 | tf_op jit(solution)/shard_map/ppermute | solution.py:12
  26.4 1.3 %collective-permute-start.5 = (f32[5,4,4,256]{3,2,1,0:T(4,128)S(1)}, f32[5,4,4,256]{3,2,1,0:T(4,128)S(1)}, u32[]{:S(2)}, u32[]{:S(2)}) collective-permute-start(f32[5,4,4,256]{3,2,1,0:T(4,128)S(1)} %get-tuple-element.8), channel_id=1, source_target_pairs={{4,0},{5,1},{6,2},{7,3},{12,8},{13,9},{14,10},{15,11},{20,16},{21,... | collective-permute-start | bytes 245768 | tf_op jit(solution)/shard_map/ppermute | solution.py:15
  27.8 4.5 %collective-permute-start = (f32[5,4,256]{2,1,0:T(4,128)S(1)}, f32[5,4,256]{2,1,0:T(4,128)S(1)}, u32[]{:S(2)}, u32[]{:S(2)}) collective-permute-start(f32[5,4,256]{2,1,0:T(4,128)S(1)} %get-tuple-element.31), channel_id=1, source_target_pairs={{0,4},{1,5},{2,6},{3,7},{8,12},{9,13},{10,14},{11,15},{16,20},{17,... | collective-permute-start | bytes 61448 | tf_op jit(solution)/shard_map/ppermute | solution.py:12
  32.3 1.3 %collective-permute-start.1 = (f32[5,4,256]{2,1,0:T(4,128)S(1)}, f32[5,4,256]{2,1,0:T(4,128)S(1)}, u32[]{:S(2)}, u32[]{:S(2)}) collective-permute-start(f32[5,4,256]{2,1,0:T(4,128)S(1)} %get-tuple-element.32), channel_id=1, source_target_pairs={{4,0},{5,1},{6,2},{7,3},{12,8},{13,9},{14,10},{15,11},{20,16},{21,... | collective-permute-start | bytes 61448 | tf_op jit(solution)/shard_map/ppermute | solution.py:15
  33.9 4.1 %collective-permute-done.1 = f32[5,4,256]{2,1,0:T(4,128)S(1)} collective-permute-done((f32[5,4,256]{2,1,0:T(4,128)S(1)}, f32[5,4,256]{2,1,0:T(4,128)S(1)}, u32[]{:S(2)}, u32[]{:S(2)}) %collective-permute-start.1) | collective-permute-done | bytes 20512 | tf_op jit(solution)/shard_map/ppermute | solution.py:15
  38.0 0.1 fusion.31
  38.1 1.3 %collective-permute-start.2 = (f32[5,40,4]{2,1,0:T(8,128)S(1)}, f32[5,40,4]{2,1,0:T(8,128)S(1)}, u32[]{:S(2)}, u32[]{:S(2)}) collective-permute-start(f32[5,40,4]{2,1,0:T(8,128)S(1)} %get-tuple-element.24), channel_id=1, source_target_pairs={{0,1},{1,2},{2,3},{4,5},{5,6},{6,7},{8,9},{9,10},{10,11},{12,13},{... | collective-permute-start | bytes 9608 | tf_op jit(solution)/shard_map/ppermute | solution.py:12
  39.4 1.3 %collective-permute-start.3 = (f32[5,40,4]{2,1,0:T(8,128)S(1)}, f32[5,40,4]{2,1,0:T(8,128)S(1)}, u32[]{:S(2)}, u32[]{:S(2)}) collective-permute-start(f32[5,40,4]{2,1,0:T(8,128)S(1)} %get-tuple-element.25), channel_id=1, source_target_pairs={{1,0},{2,1},{3,2},{5,4},{6,5},{7,6},{9,8},{10,9},{11,10},{13,12},{... | collective-permute-start | bytes 9608 | tf_op jit(solution)/shard_map/ppermute | solution.py:15
  40.8 3.6 %collective-permute-done.3 = f32[5,40,4]{2,1,0:T(8,128)S(1)} collective-permute-done((f32[5,40,4]{2,1,0:T(8,128)S(1)}, f32[5,40,4]{2,1,0:T(8,128)S(1)}, u32[]{:S(2)}, u32[]{:S(2)}) %collective-permute-start.3) | collective-permute-done | bytes 3232 | tf_op jit(solution)/shard_map/ppermute | solution.py:15
  44.4 0.2 pad_maximum_fusion.2
  44.6 0.1 slice_bitcast_fusion.13
  44.8 0.1 pad_maximum_fusion.1
  44.9 0.2 fusion.29
  45.1 5.2 %collective-permute-start.6 = (f32[5,4,40,4]{3,2,1,0:T(8,128)S(1)}, f32[5,4,40,4]{3,2,1,0:T(8,128)S(1)}, u32[]{:S(2)}, u32[]{:S(2)}) collective-permute-start(f32[5,4,40,4]{3,2,1,0:T(8,128)S(1)} %get-tuple-element.5), channel_id=1, source_target_pairs={{0,1},{1,2},{2,3},{4,5},{5,6},{6,7},{8,9},{9,10},{10,11},{12,13},{... | collective-permute-start | bytes 38408 | tf_op jit(solution)/shard_map/ppermute | solution.py:12
  50.3 1.3 %collective-permute-start.7 = (f32[5,4,40,4]{3,2,1,0:T(8,128)S(1)}, f32[5,4,40,4]{3,2,1,0:T(8,128)S(1)}, u32[]{:S(2)}, u32[]{:S(2)}) collective-permute-start(f32[5,4,40,4]{3,2,1,0:T(8,128)S(1)} %get-tuple-element.6), channel_id=1, source_target_pairs={{1,0},{2,1},{3,2},{5,4},{6,5},{7,6},{9,8},{10,9},{11,10},{13,12},{... | collective-permute-start | bytes 38408 | tf_op jit(solution)/shard_map/ppermute | solution.py:15
  51.6 0.1 slice_bitcast_fusion.14
  51.7 0.1 slice.218
  51.8 0.1 slice.225
  52.0 0.1 slice.231
  52.1 0.1 slice.216
  52.2 0.1 slice.238
  52.3 0.1 slice.244
  52.5 1.4 %collective-permute-done.7 = f32[5,4,40,4]{3,2,1,0:T(8,128)S(1)} collective-permute-done((f32[5,4,40,4]{3,2,1,0:T(8,128)S(1)}, f32[5,4,40,4]{3,2,1,0:T(8,128)S(1)}, u32[]{:S(2)}, u32[]{:S(2)}) %collective-permute-start.7) | collective-permute-done | bytes 12832 | tf_op jit(solution)/shard_map/ppermute | solution.py:15
  53.9 0.7 pad_maximum_fusion
  54.6 1.3 %fusion.11 = f32[5,4,38,262]{3,2,1,0:T(8,128)S(1)} fusion(f32[5,4,40,264]{3,2,1,0:T(8,128)S(1)} %pad_maximum_fusion, f32[38,262]{1,0:T(8,128)S(1)} %slice.234, f32[38,262]{1,0:T(8,128)S(1)} %slice.231, f32[38,262]{1,0:T(8,128)S(1)} %slice.228, f32[38,262]{1,0:T(8,128)S(1)} %slice.225, f32[38,262]{1,0:T(8,128)S(1)} %and_convert_fusion.2, f32[38,262]{1,0:T(8,128)S(1)} %slice.218), kind=kLoop, calls=%fused_computation.22 | loop fusion | flops 1991200 | bytes 5017824 | tf_op jit(solution)/shard_map/mul | solution.py:61
  55.9 1.4 %fusion.6 = f32[5,4,36,260]{3,2,1,0:T(8,128)S(1)} fusion(f32[5,4,38,262]{3,2,1,0:T(8,128)S(1)} %fusion.11, f32[36,260]{1,0:T(8,128)S(1)} %slice.247, f32[36,260]{1,0:T(8,128)S(1)} %slice.244, f32[36,260]{1,0:T(8,128)S(1)} %slice.241, f32[36,260]{1,0:T(8,128)S(1)} %slice.238, f32[36,260]{1,0:T(8,128)S(1)} %and_convert_fusion.1, f32[36,260]{1,0:T(8,128)S(1)} %slice.216), kind=kLoop, calls=%fused_computation.12 | loop fusion | flops 1872000 | bytes 4717440 | tf_op jit(solution)/shard_map/mul | solution.py:62
  57.3 1.4 %fusion.1 = f32[5,4,34,258]{3,2,1,0:T(8,128)S(1)} fusion(f32[5,4,36,260]{3,2,1,0:T(8,128)S(1)} %fusion.6, f32[34,258]{1,0:T(8,128)S(1)} %and_convert_fusion, f32[34,258]{1,0:T(8,128)S(1)} %get-tuple-element.10, f32[34,258]{1,0:T(8,128)S(1)} %get-tuple-element.11, f32[34,258]{1,0:T(8,128)S(1)} %get-tuple-element.12, f32[34,258]{1,0:T(8,128)S(1)} %get-tuple-element.13, ...), kind=kLoop, calls=%fused_computation.2 | loop fusion | flops 1754400 | bytes 4421088 | tf_op jit(solution)/shard_map/mul | solution.py:63
  58.7 1.4 %fusion.15 = f32[4,32,256]{2,1,0:T(8,128)} fusion(bf16[5,4,32,256]{3,2,1,0:T(8,128)(2,1)S(1)} %copy-done.1, f32[5,4,34,258]{3,2,1,0:T(8,128)S(1)} %fusion.1, f32[32,256]{1,0:T(8,128)S(1)} %get-tuple-element.29, f32[32,256]{1,0:T(8,128)S(1)} %get-tuple-element.30, f32[32,256]{1,0:T(8,128)S(1)} %get-tuple-element.27, f32[32,256]{1,0:T(8,128)S(1)} %get-tuple-element.28, ...), kind=kLoop, calls=%fused_computation.34 | loop fusion | flops 1933312 | bytes 3899392 | tf_op jit(solution)/shard_map/reduce_sum | solution.py:79
  60.1 24.0 %reduce-scatter.2.cloned.1.call-done = f32[1,32,256]{2,1,0:T(8,128)} async-done(((f32[4,32,256]{2,1,0:T(8,128)}), f32[1,32,256]{2,1,0:T(8,128)}) %reduce-scatter.2.cloned.1.call-update) | async-done | bytes 32784 | tf_op jit(solution)/shard_map/reduce_scatter | solution.py:80
  84.1 1.4 %broadcast_multiply_fusion = f32[1,32,256]{2,1,0:T(8,128)} fusion(f32[1,32,256]{2,1,0:T(8,128)} %reduce-scatter.2.cloned.1.call-done), kind=kLoop, calls=%fused_computation.69 | loop fusion | flops 8192 | bytes 65536 | tf_op jit(solution)/shard_map/mul | solution.py:82
  (29 shorter events, 0.6 us)
Async XLA Ops:
  6.5 21.2 %copy-start = (f32[5,32,256]{2,1,0:T(8,128)S(1)}, f32[5,32,256]{2,1,0:T(8,128)}, u32[]{:S(2)}) copy-start(f32[5,32,256]{2,1,0:T(8,128)} %param.5) | copy-start | bytes 491524
  6.5 77.6 %reduce-scatter.2.cloned.1.call-start = ((), (), s32[]{:S(2)}) async-start(), calls=%async_computation.1 | async-start | bytes 163840 | tf_op jit(solution)/shard_map/reduce_scatter | solution.py:80
  23.0 21.7 %collective-permute-start.4 = (f32[5,4,4,256]{3,2,1,0:T(4,128)S(1)}, f32[5,4,4,256]{3,2,1,0:T(4,128)S(1)}, u32[]{:S(2)}, u32[]{:S(2)}) collective-permute-start(f32[5,4,4,256]{3,2,1,0:T(4,128)S(1)} %get-tuple-element.7), channel_id=1, source_target_pairs={{0,4},{1,5},{2,6},{3,7},{8,12},{9,13},{10,14},{11,15},{16,20},{17,... | collective-permute-start | bytes 245768 | tf_op jit(solution)/shard_map/ppermute | solution.py:12
  26.4 18.3 %collective-permute-start.5 = (f32[5,4,4,256]{3,2,1,0:T(4,128)S(1)}, f32[5,4,4,256]{3,2,1,0:T(4,128)S(1)}, u32[]{:S(2)}, u32[]{:S(2)}) collective-permute-start(f32[5,4,4,256]{3,2,1,0:T(4,128)S(1)} %get-tuple-element.8), channel_id=1, source_target_pairs={{4,0},{5,1},{6,2},{7,3},{12,8},{13,9},{14,10},{15,11},{20,16},{21,... | collective-permute-start | bytes 245768 | tf_op jit(solution)/shard_map/ppermute | solution.py:15
  27.8 6.1 %collective-permute-start = (f32[5,4,256]{2,1,0:T(4,128)S(1)}, f32[5,4,256]{2,1,0:T(4,128)S(1)}, u32[]{:S(2)}, u32[]{:S(2)}) collective-permute-start(f32[5,4,256]{2,1,0:T(4,128)S(1)} %get-tuple-element.31), channel_id=1, source_target_pairs={{0,4},{1,5},{2,6},{3,7},{8,12},{9,13},{10,14},{11,15},{16,20},{17,... | collective-permute-start | bytes 61448 | tf_op jit(solution)/shard_map/ppermute | solution.py:12
  32.3 5.7 %collective-permute-start.1 = (f32[5,4,256]{2,1,0:T(4,128)S(1)}, f32[5,4,256]{2,1,0:T(4,128)S(1)}, u32[]{:S(2)}, u32[]{:S(2)}) collective-permute-start(f32[5,4,256]{2,1,0:T(4,128)S(1)} %get-tuple-element.32), channel_id=1, source_target_pairs={{4,0},{5,1},{6,2},{7,3},{12,8},{13,9},{14,10},{15,11},{20,16},{21,... | collective-permute-start | bytes 61448 | tf_op jit(solution)/shard_map/ppermute | solution.py:15
  38.1 2.7 %collective-permute-start.2 = (f32[5,40,4]{2,1,0:T(8,128)S(1)}, f32[5,40,4]{2,1,0:T(8,128)S(1)}, u32[]{:S(2)}, u32[]{:S(2)}) collective-permute-start(f32[5,40,4]{2,1,0:T(8,128)S(1)} %get-tuple-element.24), channel_id=1, source_target_pairs={{0,1},{1,2},{2,3},{4,5},{5,6},{6,7},{8,9},{9,10},{10,11},{12,13},{... | collective-permute-start | bytes 9608 | tf_op jit(solution)/shard_map/ppermute | solution.py:12
  39.4 5.0 %collective-permute-start.3 = (f32[5,40,4]{2,1,0:T(8,128)S(1)}, f32[5,40,4]{2,1,0:T(8,128)S(1)}, u32[]{:S(2)}, u32[]{:S(2)}) collective-permute-start(f32[5,40,4]{2,1,0:T(8,128)S(1)} %get-tuple-element.25), channel_id=1, source_target_pairs={{1,0},{2,1},{3,2},{5,4},{6,5},{7,6},{9,8},{10,9},{11,10},{13,12},{... | collective-permute-start | bytes 9608 | tf_op jit(solution)/shard_map/ppermute | solution.py:15
  45.1 7.4 %collective-permute-start.6 = (f32[5,4,40,4]{3,2,1,0:T(8,128)S(1)}, f32[5,4,40,4]{3,2,1,0:T(8,128)S(1)}, u32[]{:S(2)}, u32[]{:S(2)}) collective-permute-start(f32[5,4,40,4]{3,2,1,0:T(8,128)S(1)} %get-tuple-element.5), channel_id=1, source_target_pairs={{0,1},{1,2},{2,3},{4,5},{5,6},{6,7},{8,9},{9,10},{10,11},{12,13},{... | collective-permute-start | bytes 38408 | tf_op jit(solution)/shard_map/ppermute | solution.py:12
  50.3 3.6 %collective-permute-start.7 = (f32[5,4,40,4]{3,2,1,0:T(8,128)S(1)}, f32[5,4,40,4]{3,2,1,0:T(8,128)S(1)}, u32[]{:S(2)}, u32[]{:S(2)}) collective-permute-start(f32[5,4,40,4]{3,2,1,0:T(8,128)S(1)} %get-tuple-element.6), channel_id=1, source_target_pairs={{1,0},{2,1},{3,2},{5,4},{6,5},{7,6},{9,8},{10,9},{11,10},{13,12},{... | collective-permute-start | bytes 38408 | tf_op jit(solution)/shard_map/ppermute | solution.py:15
  57.3 1.4 %copy-start.1 = (bf16[5,4,32,256]{3,2,1,0:T(8,128)(2,1)S(1)}, bf16[5,4,32,256]{3,2,1,0:T(8,128)(2,1)}, u32[]{:S(2)}) copy-start(bf16[5,4,32,256]{3,2,1,0:T(8,128)(2,1)} %param.4) | copy-start | bytes 983044
Sparse Core Ops, SparseCore 0:
  60.3 23.7 reduce-scatter.1
where the time goes:
time: 92.7 us; the launch traced here: 92.3 us
  waiting for transfers between devices  33.1 us (36%)
  starting transfers between devices  19.6 us (21%)
  blocking collectives  15.4 us (17%)
  between operations  13.7 us (15%)
  other arithmetic  9.19 us (10%)
  local copies, waits for them, and re-layouts  1.32 us (1%)
    reduce_scatter x1, waiting for transfers between devices, body(): reduced = lax.psum_scatter(summed, 'mem', scatter_dimension=0, tiled=True)  24 us
    all_gather x1, blocking collectives, body(): gathered = lax.all_gather(gradient, 'mem', axis=0, tiled=True)  15.4 us
    ppermute x4, starting transfers between devices, extended(): lax.ppermute(lax.slice_in_dim(block, block.shape[dim] - width, None, axis...  14.4 us
    ppermute x4, waiting for transfers between devices, extended(): lax.ppermute(lax.slice_in_dim(block, 0, width, axis=dim), axis, backward)  9.1 us
    ppermute x4, starting transfers between devices, extended(): lax.ppermute(lax.slice_in_dim(block, 0, width, axis=dim), axis, backward)  5.17 us
  transfers between devices with their start and end apart: 9, of which 4 were waited for; matrix products, arithmetic and copies ran while one was open for 2% of the time, Pallas kernels for 0%

commit v1 on v0

v1 whole, which is shorter than its diff:
```python
import functools

import jax
import jax.numpy as jnp
from jax import lax
from jax.experimental import pallas as pl
from jax.experimental.pallas import tpu as pltpu
from jax.sharding import PartitionSpec as P

HALO = 4
LANES = 128
SUB = 8
QUAD = 4
DIRECTIONS = ((-1, 0), (1, 0), (0, -1), (0, 1), (-1, -1), (-1, 1), (1, -1), (1, 1))


def shifted(values, offset, axis):
    return pltpu.roll(values, (-offset) % values.shape[axis], axis)


def circular(centre_rows, north_rows, south_rows, row_low):
    return jnp.concatenate([centre_rows, jnp.where(row_low, south_rows, north_rows)], axis=0)


def folded(padded, cols):
    low = lax.broadcasted_iota(jnp.int32, (padded.shape[0], LANES), 1) < LANES // 2
    side = jnp.where(low, padded[:, LANES + cols :], padded[:, :LANES])
    return jnp.concatenate([padded[:, LANES : LANES + cols], side], axis=1)


def kernel(
    sizes,
    pert,
    grad,
    coef,
    out,
    centre,
    field,
    send_rows,
    send_cols,
    recv_rows,
    recv_cols,
    ext,
    stencils,
    scaled,
    z_send,
    z_recv,
    halo_send,
    halo_recv,
    local_sem,
):
    mem_count, lat_count, lon_count, scale = sizes
    per_mem, _, rows, cols = pert.shape
    members = centre.shape[0]
    mem, lat, lon = (lax.axis_index(name) for name in ("mem", "lat", "lon"))
    mesh_id = pl.DeviceIdType.MESH

    def present(direction):
        up, right = direction
        checks = []
        if up:
            checks.append(lat > 0 if up < 0 else lat < lat_count - 1)
        if right:
            checks.append(lon > 0 if right < 0 else lon < lon_count - 1)
        return functools.reduce(jnp.logical_and, checks)

    def neighbour(direction):
        return (mem, lat + direction[0], lon + direction[1])

    def peer(offset):
        return lax.rem(mem + offset, mem_count)

    barrier = pltpu.get_barrier_semaphore()
    for offset in range(1, mem_count):
        pl.semaphore_signal(barrier, inc=1, device_id=(peer(offset), lat, lon), device_id_type=mesh_id)
    for direction in DIRECTIONS:

        @pl.when(present(direction))
        def _():
            pl.semaphore_signal(barrier, inc=1, device_id=neighbour(direction), device_id_type=mesh_id)

    own_pert = pltpu.make_async_copy(
        pert.at[:, mem], centre.at[pl.ds(mem * per_mem, per_mem)], local_sem.at[0]
    )
    own_pert.start()
    inner_rows, inner_cols = pl.ds(SUB, rows), pl.ds(LANES, cols)
    own_coef = pltpu.make_async_copy(
        coef, ext.at[pl.ds(0, 5), inner_rows, inner_cols], local_sem.at[1]
    )
    own_coef.start()
    own_grad = pltpu.make_async_copy(
        grad, ext.at[pl.ds(5, 1), inner_rows, inner_cols], local_sem.at[2]
    )
    own_grad.start()

    blocks = [
        1 + jnp.where(here > 0, 1, 0) + jnp.where(here < count - 1, 1, 0)
        for here, count in ((lat, lat_count), (lon, lon_count))
    ]
    pl.semaphore_wait(barrier, mem_count - 2 + blocks[0] * blocks[1])

    def across(offset):
        target = peer(offset)
        return pltpu.make_async_remote_copy(
            src_ref=pert.at[:, target],
            dst_ref=centre.at[pl.ds(mem * per_mem, per_mem)],
            send_sem=z_send.at[offset - 1],
            recv_sem=z_recv.at[offset - 1],
            device_id=(target, lat, lon),
            device_id_type=mesh_id,
        )

    def arriving(offset):
        source = peer(mem_count - offset)
        return pltpu.make_async_remote_copy(
            src_ref=pert.at[:, source],
            dst_ref=centre.at[pl.ds(source * per_mem, per_mem)],
            send_sem=z_send.at[offset - 1],
            recv_sem=z_recv.at[offset - 1],
            device_id=(source, lat, lon),
            device_id_type=mesh_id,
        )

    for offset in range(1, mem_count):
        across(offset).start()

    def span(step, low, size, edge):
        if step == 0:
            return pl.ds(0, size), pl.ds(low, size)
        if step < 0:
            return pl.ds(0, edge), pl.ds(low + size, edge)
        return pl.ds(size - edge, edge), pl.ds(low - edge, edge)

    def fixed_copies(number, direction):
        source_rows, target_rows = span(direction[0], SUB, rows, SUB)
        source_cols, target_cols = span(direction[1], LANES, cols, LANES)
        common = dict(device_id=neighbour(direction), device_id_type=mesh_id)
        return [
            pltpu.make_async_remote_copy(
                src_ref=coef.at[:, source_rows, source_cols],
                dst_ref=ext.at[pl.ds(0, 5), target_rows, target_cols],
                send_sem=halo_send.at[0, number],
                recv_sem=halo_recv.at[0, number],
                **common,
            ),
            pltpu.make_async_remote_copy(
                src_ref=grad.at[:, source_rows, source_cols],
                dst_ref=ext.at[pl.ds(5, 1), target_rows, target_cols],
                send_sem=halo_send.at[1, number],
                recv_sem=halo_recv.at[1, number],
                **common,
            ),
        ]

    def pert_copy(number, direction):
        up, right = direction
        if up == 0:
            side = 0 if right < 0 else 1
            source, target = send_cols.at[side], recv_cols.at[side]
        else:
            side = 0 if up < 0 else 1
            source_cols, target_cols = span(right, LANES, cols, LANES)
            source = send_rows.at[side, :, source_cols]
            target = recv_rows.at[side, :, target_cols]
        return pltpu.make_async_remote_copy(
            src_ref=source,
            dst_ref=target,
            send_sem=halo_send.at[2, number],
            recv_sem=halo_recv.at[2, number],
            device_id=neighbour(direction),
            device_id_type=mesh_id,
        )

    for number, direction in enumerate(DIRECTIONS):

        @pl.when(present(direction))
        def _():
            for copy in fixed_copies(number, direction):
                copy.start()

    own_pert.wait()
    for offset in range(1, mem_count):
        arriving(offset).wait_recv()

    low_row = lax.broadcasted_iota(jnp.int32, (SUB, cols), 0) < HALO
    lane = lax.broadcasted_iota(jnp.int32, (rows, LANES), 1)

    def pack(quad, carry):
        tops, bottoms = [], []
        west = east = None
        for k in range(QUAD):
            block = centre[quad * QUAD + k].astype(jnp.float32)
            tops.append(block[:SUB])
            bottoms.append(block[rows - SUB :])
            place = (lane >= HALO * k) & (lane < HALO * (k + 1))
            first = pltpu.roll(block[:, :LANES], HALO * k, 1) if k else block[:, :LANES]
            last = pltpu.roll(block[:, cols - LANES :], HALO * (k + 1), 1)
            west = first if west is None else jnp.where(place, first, west)
            east = last if east is None else jnp.where(place, last, east)
        top_tiles = [
            jnp.where(low_row, tops[k], pltpu.roll(tops[k + 1], HALO, 0)) for k in (0, 2)
        ]
        bottom_tiles = [
            jnp.where(low_row, pltpu.roll(bottoms[k + 1], HALO, 0), bottoms[k]) for k in (0, 2)
        ]
        here = pl.ds(pl.multiple_of(quad * 2 * SUB, 2 * SUB), 2 * SUB)
        send_rows[0, here, :] = jnp.concatenate(top_tiles, axis=0).astype(jnp.bfloat16)
        send_rows[1, here, :] = jnp.concatenate(bottom_tiles, axis=0).astype(jnp.bfloat16)
        send_cols[0, quad] = west.astype(jnp.bfloat16)
        send_cols[1, quad] = east.astype(jnp.bfloat16)
        return carry

    lax.fori_loop(0, members // QUAD, pack, 0)

    for number, direction in enumerate(DIRECTIONS):

        @pl.when(present(direction))
        def _():
            pert_copy(number, direction).start()

    own_coef.wait()
    own_grad.wait()
    for number, direction in enumerate(DIRECTIONS):
        source = (-direction[0], -direction[1])

        @pl.when(present(source))
        def _():
            for copy in fixed_copies(number, direction):
                copy.wait_recv()

    full_rows, full_cols = rows + 2 * HALO, cols + LANES
    row_index = lax.broadcasted_iota(jnp.int32, (full_rows, full_cols), 0)
    col_index = lax.broadcasted_iota(jnp.int32, (full_rows, full_cols), 1)
    row_index = jnp.where(row_index < rows + HALO, row_index, row_index - full_rows)
    col_index = jnp.where(col_index < cols + LANES // 2, col_index, col_index - full_cols)
    near = (col_index >= -HALO) & (col_index < cols + HALO)
    row_index = row_index + lat * rows
    col_index = col_index + lon * cols
    inside = (
        near
        & (row_index >= 0)
        & (row_index < rows * lat_count)
        & (col_index >= 0)
        & (col_index < cols * lon_count)
    )
    low_row_full = lax.broadcasted_iota(jnp.int32, (SUB, full_cols), 0) < HALO

    def extended(index):
        wide = folded(ext[index], cols)
        wide = circular(
            wide[SUB : SUB + rows], wide[:SUB], wide[SUB + rows :], low_row_full
        )
        return jnp.where(inside, wide, 0.0)

    c0, cn, cs, cw, ce = (extended(index) for index in range(5))
    for index, value in enumerate((c0, cn, cs, cw, ce)):
        stencils[index] = value
    for index, value in enumerate(
        (shifted(cs, -1, 0), shifted(cn, 1, 0), shifted(ce, -1, 1), shifted(cw, 1, 1))
    ):
        stencils[5 + index] = jnp.where(inside, value, 0.0)
    scaled[0] = extended(5)
    scaled[1] = inside.astype(jnp.float32)

    for number, direction in enumerate(DIRECTIONS):
        source = (-direction[0], -direction[1])

        @pl.when(present(source))
        def _():
            pert_copy(number, direction).wait_recv()

    out[0] = jnp.zeros((rows, cols), jnp.float32)

    def one_pass(values, first):
        total = stencils[0] * values + stencils[first] * shifted(values, -1, 0)
        total = total + stencils[first + 1] * shifted(values, 1, 0)
        total = total + stencils[first + 2] * shifted(values, -1, 1)
        return total + stencils[first + 3] * shifted(values, 1, 1)

    def work(quad, carry):
        here = pl.ds(pl.multiple_of(quad * 2 * SUB, 2 * SUB), 2 * SUB)
        south = folded(recv_rows[0, here, :].astype(jnp.float32), cols)
        north = folded(recv_rows[1, here, :].astype(jnp.float32), cols)
        from_east = recv_cols[0, quad].astype(jnp.float32)
        from_west = recv_cols[1, quad].astype(jnp.float32)
        for k in range(QUAD):
            block = centre[quad * QUAD + k].astype(jnp.float32)
            tile = slice((k // 2) * SUB, (k // 2 + 1) * SUB)
            south_rows, north_rows = south[tile], north[tile]
            if k % 2:
                south_rows = pltpu.roll(south_rows, HALO, 0)
                north_rows = pltpu.roll(north_rows, HALO, 0)
            east = pltpu.roll(from_east, LANES - HALO * k, 1) if k else from_east
            west = pltpu.roll(from_west, LANES - HALO * (k + 1), 1)
            side = jnp.where(lane < LANES // 2, east, west)
            field[k] = circular(
                jnp.concatenate([block, side], axis=1), north_rows, south_rows, low_row_full
            )
        for k in range(QUAD):
            values = jnp.where(scaled[1] > 0.5, field[k] * scaled[0], 0.0)
            values = one_pass(values, 5)
            values = one_pass(values, 5)
            values = one_pass(values, 1)
            values = one_pass(values, 1)
            out[0] += values[:rows, :cols] * field[k, :rows, :cols]
        return carry

    lax.fori_loop(0, members // QUAD, work, 0)
    out[0] = out[0] * scale

    for offset in range(1, mem_count):
        across(offset).wait_send()
    for number, direction in enumerate(DIRECTIONS):

        @pl.when(present(direction))
        def _():
            for copy in fixed_copies(number, direction):
                copy.wait_send()
            pert_copy(number, direction).wait_send()


def body(mesh_sizes, gradient, perturbations, filter_coef):
    mem_count, lat_count, lon_count = mesh_sizes
    levels, rows, cols = gradient.shape
    members = perturbations.shape[0] * mem_count
    assert levels == 1 and members % QUAD == 0 and rows % 16 == 0 and cols % LANES == 0
    full_rows, full_cols = rows + 2 * HALO, cols + LANES
    packed = members // QUAD * 2 * SUB
    sizes = (mem_count, lat_count, lon_count, 1.0 / (members - 1))
    return pl.pallas_call(
        functools.partial(kernel, sizes),
        out_shape=jax.ShapeDtypeStruct(gradient.shape, jnp.float32),
        in_specs=[pl.BlockSpec(memory_space=pl.ANY)] * 3,
        out_specs=pl.BlockSpec(memory_space=pltpu.VMEM),
        scratch_shapes=[
            pltpu.VMEM((members, rows, cols), jnp.bfloat16),
            pltpu.VMEM((QUAD, full_rows, full_cols), jnp.float32),
            pltpu.VMEM((2, packed, cols), jnp.bfloat16),
            pltpu.VMEM((2, members // QUAD, rows, LANES), jnp.bfloat16),
            pltpu.VMEM((2, packed, cols + 2 * LANES), jnp.bfloat16),
            pltpu.VMEM((2, members // QUAD, rows, LANES), jnp.bfloat16),
            pltpu.VMEM((6, rows + 2 * SUB, cols + 2 * LANES), jnp.float32),
            pltpu.VMEM((9, full_rows, full_cols), jnp.float32),
            pltpu.VMEM((2, full_rows, full_cols), jnp.float32),
            pltpu.SemaphoreType.DMA((max(1, mem_count - 1),)),
            pltpu.SemaphoreType.DMA((max(1, mem_count - 1),)),
            pltpu.SemaphoreType.DMA((3, len(DIRECTIONS))),
            pltpu.SemaphoreType.DMA((3, len(DIRECTIONS))),
            pltpu.SemaphoreType.DMA((3,)),
        ],
        compiler_params=pltpu.CompilerParams(
            collective_id=0, has_side_effects=True, vmem_limit_bytes=32 * 1024 * 1024
        ),
    )(perturbations, gradient, filter_coef)


def solution(mesh):
    sizes = tuple(mesh.shape[name] for name in ("mem", "lat", "lon"))
    return jax.shard_map(
        functools.partial(body, sizes),
        mesh=mesh,
        in_specs=(P("mem", "lat", "lon"), P("mem", None, "lat", "lon"), P(None, "lat", "lon")),
        out_specs=P("mem", "lat", "lon"),
        check_vma=False,
    )
```

time: 92.7 us -> 25.2 us (0.27)
  waiting for transfers between devices: 33.1 us -> 0 us
  Pallas kernels: 0 us -> 21.6 us
  starting transfers between devices: 19.6 us -> 0 us
  blocking collectives: 15.4 us -> 0 us
  between operations: 13.7 us -> 0.01 us
  other arithmetic: 9.19 us -> 0 us
  local copies, waits for them, and re-layouts: 1.32 us -> 3.26 us
    reduce_scatter x1 -> x0, waiting for transfers between devices: 24 us -> none  [body(): reduced = lax.psum_scatter(summed, 'mem', scatter_dimension=0, tiled=True)]
    pallas_call x0 -> x1, Pallas kernels: none -> 21.6 us  [body(): pl.pallas_call(functools.partial(kernel, sizes), out_shape=jax.ShapeDtype...]
    ppermute x8 -> x0, starting transfers between devices: 19.6 us -> none  [the longest x4 14.4 us: extended(): lax.ppermute(lax.slice_in_dim(block, block.shape[dim] - width, None, axis...]
    all_gather x1 -> x0, blocking collectives: 15.4 us -> none  [body(): gathered = lax.all_gather(gradient, 'mem', axis=0, tiled=True)]
    ppermute x8 -> x0, waiting for transfers between devices: 9.11 us -> none  [the longest x4 9.1 us: extended(): lax.ppermute(lax.slice_in_dim(block, 0, width, axis=dim), axis, backward)]
    mul x5 -> x0, other arithmetic: 6.48 us -> none  [the longest x1 1.38 us: body(): return reduced * (1.0 / (member_count - 1))]
    unnamed x4 -> x7, local copies, waits for them, and re-layouts: 0.01 us -> 3.26 us
    reduce_sum x1 -> x0, other arithmetic: 1.42 us -> none  [body(): summed = jnp.sum(member_vals * filtered, axis=0)]
  transfers between devices with their start and end apart: 9 -> 0, of which waited for: 4 -> 0; matrix products, arithmetic and copies ran while one was open for 2% -> 0% of each run, Pallas kernels for 0% -> 0%
where the time goes in v1:
time: 25.2 us; the launch traced here: 24.8 us
  Pallas kernels  21.6 us (86%)
  local copies, waits for them, and re-layouts  3.26 us (13%)
    pallas_call x1, Pallas kernels, body(): pl.pallas_call(functools.partial(kernel, sizes), out_shape=jax.ShapeDtype...  21.6 us
    unnamed x7, local copies, waits for them, and re-layouts  3.26 us

profile of v1, /device:TPU:0, one launch (start us, length us, event | category | flops | bytes accessed | tf_op | source)
XLA Modules:
  0.0 24.8 jit_solution(454625187871508420)
XLA Ops:
  0.0 0.0 copy-start
  0.0 1.0 %copy-done = bf16[5,4,32,256]{3,2,1,0:T(8,128)(2,1)S(1)} copy-done((bf16[5,4,32,256]{3,2,1,0:T(8,128)(2,1)S(1)}, bf16[5,4,32,256]{3,2,1,0:T(8,128)(2,1)}, u32[]{:S(2)}) %copy-start) | copy-done | bytes 327704
  1.0 0.0 copy-start.1
  1.0 0.9 %copy-done.1 = f32[5,32,256]{2,1,0:T(8,128)S(1)} copy-done((f32[5,32,256]{2,1,0:T(8,128)S(1)}, f32[5,32,256]{2,1,0:T(8,128)}, u32[]{:S(2)}) %copy-start.1) | copy-done | bytes 163864
  1.9 0.0 copy-start.2
  1.9 0.8 %copy-done.2 = f32[1,32,256]{2,1,0:T(8,128)S(1)} copy-done((f32[1,32,256]{2,1,0:T(8,128)S(1)}, f32[1,32,256]{2,1,0:T(8,128)}, u32[]{:S(2)}) %copy-start.2) | copy-done | bytes 32792
  2.6 21.6 %shard_map.37 = f32[1,32,256]{2,1,0:T(8,128)S(1)} custom-call(bf16[5,4,32,256]{3,2,1,0:T(8,128)(2,1)S(1)} %copy-done, f32[1,32,256]{2,1,0:T(8,128)S(1)} %copy-done.2, f32[5,32,256]{2,1,0:T(8,128)S(1)} %copy-done.1), custom_call_target="tpu_custom_call" | custom-call | tf_op jit(solution)/shard_map/pallas_call | solution.py:330
  24.2 0.6 %copy.5 = f32[1,32,256]{2,1,0:T(8,128)} copy(f32[1,32,256]{2,1,0:T(8,128)S(1)} %shard_map.37) | data formatting | bytes 65536
Async XLA Ops:
  0.0 1.0 %copy-start = (bf16[5,4,32,256]{3,2,1,0:T(8,128)(2,1)S(1)}, bf16[5,4,32,256]{3,2,1,0:T(8,128)(2,1)}, u32[]{:S(2)}) copy-start(bf16[5,4,32,256]{3,2,1,0:T(8,128)(2,1)} %pert.1) | copy-start | bytes 983044
  1.0 0.9 %copy-start.1 = (f32[5,32,256]{2,1,0:T(8,128)S(1)}, f32[5,32,256]{2,1,0:T(8,128)}, u32[]{:S(2)}) copy-start(f32[5,32,256]{2,1,0:T(8,128)} %coef.1) | copy-start | bytes 491524
  1.9 0.8 %copy-start.2 = (f32[1,32,256]{2,1,0:T(8,128)S(1)}, f32[1,32,256]{2,1,0:T(8,128)}, u32[]{:S(2)}) copy-start(f32[1,32,256]{2,1,0:T(8,128)} %grad.1) | copy-start | bytes 98308

commit v2 on v1

--- a/solution.py
+++ b/solution.py
@@ -10,7 +10,6 @@
 HALO = 4
 LANES = 128
 SUB = 8
-QUAD = 4
 DIRECTIONS = ((-1, 0), (1, 0), (0, -1), (0, 1), (-1, -1), (-1, 1), (1, -1), (1, 1))
 
 
@@ -51,7 +50,6 @@
 ):
     mem_count, lat_count, lon_count, scale = sizes
     per_mem, _, rows, cols = pert.shape
-    members = centre.shape[0]
     mem, lat, lon = (lax.axis_index(name) for name in ("mem", "lat", "lon"))
     mesh_id = pl.DeviceIdType.MESH
 
@@ -68,11 +66,20 @@
         return (mem, lat + direction[0], lon + direction[1])
 
     def peer(offset):
-        return lax.rem(mem + offset, mem_count)
+        total, bit = 0, 1
+        while bit < mem_count:
+            total = total + bit * lax.rem(lax.div(mem, bit) + lax.div(offset, bit), 2)
+            bit *= 2
+        return total
+
+    def group_at(step):
+        if mem_count < 3:
+            return step
+        return jnp.where(step == 0, 0, lax.rem(step, mem_count - 1) + 1)
 
     barrier = pltpu.get_barrier_semaphore()
     for offset in range(1, mem_count):
-        pl.semaphore_signal(barrier, inc=1, device_id=(peer(offset), lat, lon), device_id_type=mesh_id)
+        pl.semaphore_signal(barrier, inc=1, device_id=(peer(jnp.int32(offset)), lat, lon), device_id_type=mesh_id)
     for direction in DIRECTIONS:
 
         @pl.when(present(direction))
@@ -80,7 +87,7 @@
             pl.semaphore_signal(barrier, inc=1, device_id=neighbour(direction), device_id_type=mesh_id)
 
     own_pert = pltpu.make_async_copy(
-        pert.at[:, mem], centre.at[pl.ds(mem * per_mem, per_mem)], local_sem.at[0]
+        pert.at[:, mem], centre.at[0], local_sem.at[0]
     )
     own_pert.start()
     inner_rows, inner_cols = pl.ds(SUB, rows), pl.ds(LANES, cols)
@@ -103,26 +110,15 @@
         target = peer(offset)
         return pltpu.make_async_remote_copy(
             src_ref=pert.at[:, target],
-            dst_ref=centre.at[pl.ds(mem * per_mem, per_mem)],
-            send_sem=z_send.at[offset - 1],
-            recv_sem=z_recv.at[offset - 1],
+            dst_ref=centre.at[offset],
+            send_sem=z_send.at[offset],
+            recv_sem=z_recv.at[offset],
             device_id=(target, lat, lon),
             device_id_type=mesh_id,
         )
 
-    def arriving(offset):
-        source = peer(mem_count - offset)
-        return pltpu.make_async_remote_copy(
-            src_ref=pert.at[:, source],
-            dst_ref=centre.at[pl.ds(source * per_mem, per_mem)],
-            send_sem=z_send.at[offset - 1],
-            recv_sem=z_recv.at[offset - 1],
-            device_id=(source, lat, lon),
-            device_id_type=mesh_id,
-        )
-
-    for offset in range(1, mem_count):
-        across(offset).start()
+    for step in range(1, mem_count):
+        across(group_at(jnp.int32(step))).start()
 
     def span(step, low, size, edge):
         if step == 0:
@@ -152,21 +148,21 @@
             ),
         ]
 
-    def pert_copy(number, direction):
+    def pert_copy(group, number, direction):
         up, right = direction
         if up == 0:
             side = 0 if right < 0 else 1
-            source, target = send_cols.at[side], recv_cols.at[side]
+            source, target = send_cols.at[group, side], recv_cols.at[group, side]
         else:
             side = 0 if up < 0 else 1
             source_cols, target_cols = span(right, LANES, cols, LANES)
-            source = send_rows.at[side, :, source_cols]
-            target = recv_rows.at[side, :, target_cols]
+            source = send_rows.at[group, side, :, source_cols]
+            target = recv_rows.at[group, side, :, target_cols]
         return pltpu.make_async_remote_copy(
             src_ref=source,
             dst_ref=target,
-            send_sem=halo_send.at[2, number],
-            recv_sem=halo_recv.at[2, number],
+            send_sem=halo_send.at[2 + group, number],
+            recv_sem=halo_recv.at[2 + group, number],
             device_id=neighbour(direction),
             device_id_type=mesh_id,
         )
@@ -178,45 +174,42 @@
             for copy in fixed_copies(number, direction):
                 copy.start()
 
-    own_pert.wait()
-    for offset in range(1, mem_count):
-        arriving(offset).wait_recv()
-
     low_row = lax.broadcasted_iota(jnp.int32, (SUB, cols), 0) < HALO
     lane = lax.broadcasted_iota(jnp.int32, (rows, LANES), 1)
-
-    def pack(quad, carry):
+    tiles = send_rows.shape[2] // SUB
+
+    def pack(group):
         tops, bottoms = [], []
         west = east = None
-        for k in range(QUAD):
-            block = centre[quad * QUAD + k].astype(jnp.float32)
-            tops.append(block[:SUB])
-            bottoms.append(block[rows - SUB :])
+        for k in range(per_mem):
+            block = centre[group, k].astype(jnp.float32)
+            top, bottom = block[:SUB], block[rows - SUB :]
+            if k % 2:
+                tops[-1] = jnp.where(low_row, tops[-1], pltpu.roll(top, HALO, 0))
+                bottoms[-1] = jnp.where(low_row, pltpu.roll(bottom, HALO, 0), bottoms[-1])
+            else:
+                tops.append(top)
+                bottoms.append(bottom)
             place = (lane >= HALO * k) & (lane < HALO * (k + 1))
             first = pltpu.roll(block[:, :LANES], HALO * k, 1) if k else block[:, :LANES]
-            last = pltpu.roll(block[:, cols - LANES :], HALO * (k + 1), 1)
+            last = pltpu.roll(block[:, cols - LANES :], HALO * (k + 1) % LANES, 1)
             west = first if west is None else jnp.where(place, first, west)
             east = last if east is None else jnp.where(place, last, east)
-        top_tiles = [
-            jnp.where(low_row, tops[k], pltpu.roll(tops[k + 1], HALO, 0)) for k in (0, 2)
-        ]
-        bottom_tiles = [
-            jnp.where(low_row, pltpu.roll(bottoms[k + 1], HALO, 0), bottoms[k]) for k in (0, 2)
-        ]
-        here = pl.ds(pl.multiple_of(quad * 2 * SUB, 2 * SUB), 2 * SUB)
-        send_rows[0, here, :] = jnp.concatenate(top_tiles, axis=0).astype(jnp.bfloat16)
-        send_rows[1, here, :] = jnp.concatenate(bottom_tiles, axis=0).astype(jnp.bfloat16)
-        send_cols[0, quad] = west.astype(jnp.bfloat16)
-        send_cols[1, quad] = east.astype(jnp.bfloat16)
-        return carry
-
-    lax.fori_loop(0, members // QUAD, pack, 0)
-
-    for number, direction in enumerate(DIRECTIONS):
-
-        @pl.when(present(direction))
-        def _():
-            pert_copy(number, direction).start()
+        while len(tops) < tiles:
+            tops.append(tops[-1])
+            bottoms.append(bottoms[-1])
+        send_rows[group, 0] = jnp.concatenate(tops, axis=0).astype(jnp.bfloat16)
+        send_rows[group, 1] = jnp.concatenate(bottoms, axis=0).astype(jnp.bfloat16)
+        send_cols[group, 0] = west.astype(jnp.bfloat16)
+        send_cols[group, 1] = east.astype(jnp.bfloat16)
+        for number, direction in enumerate(DIRECTIONS):
+
+            @pl.when(present(direction))
+            def _():
+                pert_copy(group, number, direction).start()
+
+    own_pert.wait()
+    pack(jnp.int32(0))
 
     own_coef.wait()
     own_grad.wait()
@@ -262,13 +255,6 @@
     scaled[0] = extended(5)
     scaled[1] = inside.astype(jnp.float32)
 
-    for number, direction in enumerate(DIRECTIONS):
-        source = (-direction[0], -direction[1])
-
-        @pl.when(present(source))
-        def _():
-            pert_copy(number, direction).wait_recv()
-
     out[0] = jnp.zeros((rows, cols), jnp.float32)
 
     def one_pass(values, first):
@@ -277,75 +263,93 @@
         total = total + stencils[first + 2] * shifted(values, -1, 1)
         return total + stencils[first + 3] * shifted(values, 1, 1)
 
-    def work(quad, carry):
-        here = pl.ds(pl.multiple_of(quad * 2 * SUB, 2 * SUB), 2 * SUB)
-        south = folded(recv_rows[0, here, :].astype(jnp.float32), cols)
-        north = folded(recv_rows[1, here, :].astype(jnp.float32), cols)
-        from_east = recv_cols[0, quad].astype(jnp.float32)
-        from_west = recv_cols[1, quad].astype(jnp.float32)
-        for k in range(QUAD):
-            block = centre[quad * QUAD + k].astype(jnp.float32)
+    def work(group):
+        for number, direction in enumerate(DIRECTIONS):
+            source = (-direction[0], -direction[1])
+
+            @pl.when(present(source))
+            def _():
+                pert_copy(group, number, direction).wait_recv()
+
+        south = folded(recv_rows[group, 0].astype(jnp.float32), cols)
+        north = folded(recv_rows[group, 1].astype(jnp.float32), cols)
+        from_east = recv_cols[group, 0].astype(jnp.float32)
+        from_west = recv_cols[group, 1].astype(jnp.float32)
+        for k in range(per_mem):
+            block = centre[group, k].astype(jnp.float32)
             tile = slice((k // 2) * SUB, (k // 2 + 1) * SUB)
             south_rows, north_rows = south[tile], north[tile]
             if k % 2:
                 south_rows = pltpu.roll(south_rows, HALO, 0)
                 north_rows = pltpu.roll(north_rows, HALO, 0)
             east = pltpu.roll(from_east, LANES - HALO * k, 1) if k else from_east
-            west = pltpu.roll(from_west, LANES - HALO * (k + 1), 1)
+            west = pltpu.roll(from_west, (-HALO * (k + 1)) % LANES, 1)
             side = jnp.where(lane < LANES // 2, east, west)
             field[k] = circular(
                 jnp.concatenate([block, side], axis=1), north_rows, south_rows, low_row_full
             )
-        for k in range(QUAD):
+        for k in range(per_mem):
             values = jnp.where(scaled[1] > 0.5, field[k] * scaled[0], 0.0)
             values = one_pass(values, 5)
             values = one_pass(values, 5)
             values = one_pass(values, 1)
             values = one_pass(values, 1)
             out[0] += values[:rows, :cols] * field[k, :rows, :cols]
+
+    def step_work(step, carry):
+        @pl.when(step + 1 < mem_count)
+        def _():
+            arriving = group_at(step + 1)
+            across(arriving).wait_recv()
+            pack(arriving)
+
+        work(group_at(step))
         return carry
 
-    lax.fori_loop(0, members // QUAD, work, 0)
+    lax.fori_loop(0, mem_count, step_work, 0)
     out[0] = out[0] * scale
 
     for offset in range(1, mem_count):
-        across(offset).wait_send()
+        across(jnp.int32(offset)).wait_send()
     for number, direction in enumerate(DIRECTIONS):
 
         @pl.when(present(direction))
         def _():
             for copy in fixed_copies(number, direction):
                 copy.wait_send()
-            pert_copy(number, direction).wait_send()
+            for group in range(mem_count):
+                pert_copy(jnp.int32(group), number, direction).wait_send()
 
 
 def body(mesh_sizes, gradient, perturbations, filter_coef):
     mem_count, lat_count, lon_count = mesh_sizes
     levels, rows, cols = gradient.shape
-    members = perturbations.shape[0] * mem_count
-    assert levels == 1 and members % QUAD == 0 and rows % 16 == 0 and cols % LANES == 0
+    per_mem = perturbations.shape[0]
+    members = per_mem * mem_count
+    assert mem_count & (mem_count - 1) == 0 and HALO * per_mem <= LANES
+    assert levels == 1 and rows % 16 == 0 and cols % LANES == 0
     full_rows, full_cols = rows + 2 * HALO, cols + LANES
-    packed = members // QUAD * 2 * SUB
+    packed = (per_mem + 3) // 4 * 2 * SUB
     sizes = (mem_count, lat_count, lon_count, 1.0 / (members - 1))
     return pl.pallas_call(
         functools.partial(kernel, sizes),
         out_shape=jax.ShapeDtypeStruct(gradient.shape, jnp.float32),
-        in_specs=[pl.BlockSpec(memory_space=pl.ANY)] * 3,
+        in_specs=[pl.BlockSpec(memory_space=pltpu.HBM)] * 3,
         out_specs=pl.BlockSpec(memory_space=pltpu.VMEM),
         scratch_shapes=[
-            pltpu.VMEM((members, rows, cols), jnp.bfloat16),
-            pltpu.VMEM((QUAD, full_rows, full_cols), jnp.float32),
-            pltpu.VMEM((2, packed, cols), jnp.bfloat16),
-            pltpu.VMEM((2, members // QUAD, rows, LANES), jnp.bfloat16),
-            pltpu.VMEM((2, packed, cols + 2 * LANES), jnp.bfloat16),
-            pltpu.VMEM((2, members // QUAD, rows, LANES), jnp.bfloat16),
+            pltpu.VMEM((mem_count, per_mem, rows, cols), jnp.bfloat16),
+            pltpu.VMEM((per_mem, full_rows, full_cols), jnp.float32),
+            pltpu.VMEM((mem_count, 2, packed, cols), jnp.bfloat16),
+            pltpu.VMEM((mem_count, 2, rows, LANES), jnp.bfloat16),
+            pltpu.VMEM((mem_count, 2, packed, cols + 2 * LANES), jnp.bfloat16),
+            pltpu.VMEM((mem_count, 2, rows, LANES), jnp.bfloat16),
             pltpu.VMEM((6, rows + 2 * SUB, cols + 2 * LANES), jnp.float32),
             pltpu.VMEM((9, full_rows, full_cols), jnp.float32),
             pltpu.VMEM((2, full_rows, full_cols), jnp.float32),
-            pltpu.SemaphoreType.DMA((max(1, mem_count - 1),)),
-            pltpu.SemaphoreType.DMA((max(1, mem_count - 1),)),
-            pltpu.SemaphoreType.DMA((3, len(DIRECTIONS))),
-            pltpu.SemaphoreType.DMA((3, len(DIRECTIONS))),
+            pltpu.SemaphoreType.DMA((mem_count,)),
+            pltpu.SemaphoreType.DMA((mem_count,)),
+            pltpu.SemaphoreType.DMA((2 + mem_count, len(DIRECTIONS))),
+            pltpu.SemaphoreType.DMA((2 + mem_count, len(DIRECTIONS))),
             pltpu.SemaphoreType.DMA((3,)),
         ],
         compiler_params=pltpu.CompilerParams(

time: 25.2 us -> 25.6 us (1.016)
  Pallas kernels: 21.6 us -> 21.9 us
    pallas_call x1, Pallas kernels: 21.6 us -> 21.9 us  [body(): pl.pallas_call(functools.partial(kernel, sizes), out_shape=jax.ShapeDtype...]
where the time goes in v2:
time: 25.6 us; the launch traced here: 25.2 us
  Pallas kernels  21.9 us (86%)
  local copies, waits for them, and re-layouts  3.26 us (13%)
    pallas_call x1, Pallas kernels, body(): pl.pallas_call(functools.partial(kernel, sizes), out_shape=jax.ShapeDtype...  21.9 us
    unnamed x7, local copies, waits for them, and re-layouts  3.26 us

profile of v2, /device:TPU:0, one launch (start us, length us, event | category | flops | bytes accessed | tf_op | source)
XLA Modules:
  0.0 25.2 jit_solution(14733539422310865536)
XLA Ops:
  0.0 0.0 copy-start
  0.0 1.0 %copy-done = bf16[5,4,32,256]{3,2,1,0:T(8,128)(2,1)S(1)} copy-done((bf16[5,4,32,256]{3,2,1,0:T(8,128)(2,1)S(1)}, bf16[5,4,32,256]{3,2,1,0:T(8,128)(2,1)}, u32[]{:S(2)}) %copy-start) | copy-done | bytes 327704
  1.0 0.0 copy-start.1
  1.0 0.9 %copy-done.1 = f32[5,32,256]{2,1,0:T(8,128)S(1)} copy-done((f32[5,32,256]{2,1,0:T(8,128)S(1)}, f32[5,32,256]{2,1,0:T(8,128)}, u32[]{:S(2)}) %copy-start.1) | copy-done | bytes 163864
  1.9 0.0 copy-start.2
  1.9 0.8 %copy-done.2 = f32[1,32,256]{2,1,0:T(8,128)S(1)} copy-done((f32[1,32,256]{2,1,0:T(8,128)S(1)}, f32[1,32,256]{2,1,0:T(8,128)}, u32[]{:S(2)}) %copy-start.2) | copy-done | bytes 32792
  2.6 21.9 %shard_map.37 = f32[1,32,256]{2,1,0:T(8,128)S(1)} custom-call(bf16[5,4,32,256]{3,2,1,0:T(8,128)(2,1)S(1)} %copy-done, f32[1,32,256]{2,1,0:T(8,128)S(1)} %copy-done.2, f32[5,32,256]{2,1,0:T(8,128)S(1)} %copy-done.1), custom_call_target="tpu_custom_call" | custom-call | tf_op jit(solution)/shard_map/pallas_call | solution.py:334
  24.5 0.6 %copy.5 = f32[1,32,256]{2,1,0:T(8,128)} copy(f32[1,32,256]{2,1,0:T(8,128)S(1)} %shard_map.37) | data formatting | bytes 65536
Async XLA Ops:
  0.0 1.0 %copy-start = (bf16[5,4,32,256]{3,2,1,0:T(8,128)(2,1)S(1)}, bf16[5,4,32,256]{3,2,1,0:T(8,128)(2,1)}, u32[]{:S(2)}) copy-start(bf16[5,4,32,256]{3,2,1,0:T(8,128)(2,1)} %pert.1) | copy-start | bytes 983044
  1.0 0.9 %copy-start.1 = (f32[5,32,256]{2,1,0:T(8,128)S(1)}, f32[5,32,256]{2,1,0:T(8,128)}, u32[]{:S(2)}) copy-start(f32[5,32,256]{2,1,0:T(8,128)} %coef.1) | copy-start | bytes 491524
  1.9 0.8 %copy-start.2 = (f32[1,32,256]{2,1,0:T(8,128)S(1)}, f32[1,32,256]{2,1,0:T(8,128)}, u32[]{:S(2)}) copy-start(f32[1,32,256]{2,1,0:T(8,128)} %grad.1) | copy-start | bytes 98308

commit v3 on v2

--- a/solution.py
+++ b/solution.py
@@ -42,8 +42,14 @@
     ext,
     stencils,
     scaled,
+    grads,
+    sums,
     z_send,
     z_recv,
+    sum_send,
+    sum_recv,
+    grad_send,
+    grad_recv,
     halo_send,
     halo_recv,
     local_sem,
@@ -73,9 +79,7 @@
         return total
 
     def group_at(step):
-        if mem_count < 3:
-            return step
-        return jnp.where(step == 0, 0, lax.rem(step, mem_count - 1) + 1)
+        return lax.rem(step + 1, mem_count)
 
     barrier = pltpu.get_barrier_semaphore()
     for offset in range(1, mem_count):
@@ -86,19 +90,21 @@
         def _():
             pl.semaphore_signal(barrier, inc=1, device_id=neighbour(direction), device_id_type=mesh_id)
 
-    own_pert = pltpu.make_async_copy(
-        pert.at[:, mem], centre.at[0], local_sem.at[0]
+    inner_rows, inner_cols = pl.ds(SUB, rows), pl.ds(LANES, cols)
+
+    def own_pert(group):
+        return pltpu.make_async_copy(pert.at[:, peer(group)], centre.at[group], local_sem.at[2 + group])
+
+    own_grad = pltpu.make_async_copy(
+        grad.at[0], grads.at[0, inner_rows, inner_cols], local_sem.at[0]
     )
-    own_pert.start()
-    inner_rows, inner_cols = pl.ds(SUB, rows), pl.ds(LANES, cols)
     own_coef = pltpu.make_async_copy(
-        coef, ext.at[pl.ds(0, 5), inner_rows, inner_cols], local_sem.at[1]
+        coef, ext.at[:, inner_rows, inner_cols], local_sem.at[1]
     )
+    for step in range(mem_count):
+        own_pert(group_at(jnp.int32(step))).start()
+    own_grad.start()
     own_coef.start()
-    own_grad = pltpu.make_async_copy(
-        grad, ext.at[pl.ds(5, 1), inner_rows, inner_cols], local_sem.at[2]
-    )
-    own_grad.start()
 
     blocks = [
         1 + jnp.where(here > 0, 1, 0) + jnp.where(here < count - 1, 1, 0)
@@ -107,18 +113,27 @@
     pl.semaphore_wait(barrier, mem_count - 2 + blocks[0] * blocks[1])
 
     def across(offset):
-        target = peer(offset)
         return pltpu.make_async_remote_copy(
-            src_ref=pert.at[:, target],
-            dst_ref=centre.at[offset],
+            src_ref=grad.at[0],
+            dst_ref=grads.at[offset, inner_rows, inner_cols],
             send_sem=z_send.at[offset],
             recv_sem=z_recv.at[offset],
-            device_id=(target, lat, lon),
+            device_id=(peer(offset), lat, lon),
             device_id_type=mesh_id,
         )
 
-    for step in range(1, mem_count):
-        across(group_at(jnp.int32(step))).start()
+    def back(offset):
+        return pltpu.make_async_remote_copy(
+            src_ref=sums.at[0, offset],
+            dst_ref=sums.at[1, offset],
+            send_sem=sum_send.at[offset],
+            recv_sem=sum_recv.at[offset],
+            device_id=(peer(offset), lat, lon),
+            device_id_type=mesh_id,
+        )
+
+    for offset in range(1, mem_count):
+        across(jnp.int32(offset)).start()
 
     def span(step, low, size, edge):
         if step == 0:
@@ -127,26 +142,45 @@
             return pl.ds(0, edge), pl.ds(low + size, edge)
         return pl.ds(size - edge, edge), pl.ds(low - edge, edge)
 
-    def fixed_copies(number, direction):
+    def coef_copy(number, direction):
         source_rows, target_rows = span(direction[0], SUB, rows, SUB)
         source_cols, target_cols = span(direction[1], LANES, cols, LANES)
-        common = dict(device_id=neighbour(direction), device_id_type=mesh_id)
-        return [
-            pltpu.make_async_remote_copy(
-                src_ref=coef.at[:, source_rows, source_cols],
-                dst_ref=ext.at[pl.ds(0, 5), target_rows, target_cols],
-                send_sem=halo_send.at[0, number],
-                recv_sem=halo_recv.at[0, number],
-                **common,
-            ),
-            pltpu.make_async_remote_copy(
-                src_ref=grad.at[:, source_rows, source_cols],
-                dst_ref=ext.at[pl.ds(5, 1), target_rows, target_cols],
-                send_sem=halo_send.at[1, number],
-                recv_sem=halo_recv.at[1, number],
-                **common,
-            ),
-        ]
+        return pltpu.make_async_remote_copy(
+            src_ref=coef.at[:, source_rows, source_cols],
+            dst_ref=ext.at[:, target_rows, target_cols],
+            send_sem=halo_send.at[mem_count, number],
+            recv_sem=halo_recv.at[mem_count, number],
+            device_id=neighbour(direction),
+            device_id_type=mesh_id,
+        )
+
+    def grad_copy(group, number, direction):
+        source_rows, target_rows = span(direction[0], SUB, rows, SUB)
+        source_cols, target_cols = span(direction[1], LANES, cols, LANES)
+        source_rows = pl.ds(source_rows.start + SUB, source_rows.size)
+        source_cols = pl.ds(source_cols.start + LANES, source_cols.size)
+        return pltpu.make_async_remote_copy(
+            src_ref=grads.at[group, source_rows, source_cols],
+            dst_ref=grads.at[group, target_rows, target_cols],
+            send_sem=grad_send.at[group, number],
+            recv_sem=grad_recv.at[group, number],
+            device_id=neighbour(direction),
+            device_id_type=mesh_id,
+        )
+
+    def for_targets(action):
+        for number, direction in enumerate(DIRECTIONS):
+
+            @pl.when(present(direction))
+            def _():
+                action(number, direction)
+
+    def for_sources(action):
+        for number, direction in enumerate(DIRECTIONS):
+
+            @pl.when(present((-direction[0], -direction[1])))
+            def _():
+                action(number, direction)
 
     def pert_copy(group, number, direction):
         up, right = direction
@@ -161,18 +195,13 @@
         return pltpu.make_async_remote_copy(
             src_ref=source,
             dst_ref=target,
-            send_sem=halo_send.at[2 + group, number],
-            recv_sem=halo_recv.at[2 + group, number],
+            send_sem=halo_send.at[group, number],
+            recv_sem=halo_recv.at[group, number],
             device_id=neighbour(direction),
             device_id_type=mesh_id,
         )
 
-    for number, direction in enumerate(DIRECTIONS):
-
-        @pl.when(present(direction))
-        def _():
-            for copy in fixed_copies(number, direction):
-                copy.start()
+    for_targets(lambda number, direction: coef_copy(number, direction).start())
 
     low_row = lax.broadcasted_iota(jnp.int32, (SUB, cols), 0) < HALO
     lane = lax.broadcasted_iota(jnp.int32, (rows, LANES), 1)
@@ -202,24 +231,22 @@
         send_rows[group, 1] = jnp.concatenate(bottoms, axis=0).astype(jnp.bfloat16)
         send_cols[group, 0] = west.astype(jnp.bfloat16)
         send_cols[group, 1] = east.astype(jnp.bfloat16)
-        for number, direction in enumerate(DIRECTIONS):
-
-            @pl.when(present(direction))
-            def _():
-                pert_copy(group, number, direction).start()
-
-    own_pert.wait()
-    pack(jnp.int32(0))
-
+        for_targets(lambda number, direction: pert_copy(group, number, direction).start())
+
+    def forward(group):
+        for_targets(lambda number, direction: grad_copy(group, number, direction).start())
+
+    def pack_step(step, carry):
+        group = group_at(step)
+        own_pert(group).wait()
+        pack(group)
+        return carry
+
+    lax.fori_loop(0, mem_count, pack_step, 0)
+    own_grad.wait()
+    forward(jnp.int32(0))
     own_coef.wait()
-    own_grad.wait()
-    for number, direction in enumerate(DIRECTIONS):
-        source = (-direction[0], -direction[1])
-
-        @pl.when(present(source))
-        def _():
-            for copy in fixed_copies(number, direction):
-                copy.wait_recv()
+    for_sources(lambda number, direction: coef_copy(number, direction).wait_recv())
 
     full_rows, full_cols = rows + 2 * HALO, cols + LANES
     row_index = lax.broadcasted_iota(jnp.int32, (full_rows, full_cols), 0)
@@ -238,24 +265,21 @@
     )
     low_row_full = lax.broadcasted_iota(jnp.int32, (SUB, full_cols), 0) < HALO
 
-    def extended(index):
-        wide = folded(ext[index], cols)
+    def extended(block):
+        wide = folded(block, cols)
         wide = circular(
             wide[SUB : SUB + rows], wide[:SUB], wide[SUB + rows :], low_row_full
         )
         return jnp.where(inside, wide, 0.0)
 
-    c0, cn, cs, cw, ce = (extended(index) for index in range(5))
+    c0, cn, cs, cw, ce = (extended(ext[index]) for index in range(5))
     for index, value in enumerate((c0, cn, cs, cw, ce)):
         stencils[index] = value
     for index, value in enumerate(
         (shifted(cs, -1, 0), shifted(cn, 1, 0), shifted(ce, -1, 1), shifted(cw, 1, 1))
     ):
         stencils[5 + index] = jnp.where(inside, value, 0.0)
-    scaled[0] = extended(5)
     scaled[1] = inside.astype(jnp.float32)
-
-    out[0] = jnp.zeros((rows, cols), jnp.float32)
 
     def one_pass(values, first):
         total = stencils[0] * values + stencils[first] * shifted(values, -1, 0)
@@ -264,13 +288,10 @@
         return total + stencils[first + 3] * shifted(values, 1, 1)
 
     def work(group):
-        for number, direction in enumerate(DIRECTIONS):
-            source = (-direction[0], -direction[1])
-
-            @pl.when(present(source))
-            def _():
-                pert_copy(group, number, direction).wait_recv()
-
+        for_sources(lambda number, direction: pert_copy(group, number, direction).wait_recv())
+        for_sources(lambda number, direction: grad_copy(group, number, direction).wait_recv())
+        scaled[0] = extended(grads[group])
+        total = jnp.zeros((rows, cols), jnp.float32)
         south = folded(recv_rows[group, 0].astype(jnp.float32), cols)
         north = folded(recv_rows[group, 1].astype(jnp.float32), cols)
         from_east = recv_cols[group, 0].astype(jnp.float32)
@@ -294,31 +315,42 @@
             values = one_pass(values, 5)
             values = one_pass(values, 1)
             values = one_pass(values, 1)
-            out[0] += values[:rows, :cols] * field[k, :rows, :cols]
+            total = total + values[:rows, :cols] * field[k, :rows, :cols]
+        sums[0, group] = total
+
+    if mem_count > 1:
+        across(jnp.int32(1)).wait_recv()
+        forward(jnp.int32(1))
 
     def step_work(step, carry):
+        @pl.when(step + 2 < mem_count)
+        def _():
+            across(step + 2).wait_recv()
+            forward(step + 2)
+
+        group = group_at(step)
+        work(group)
+
         @pl.when(step + 1 < mem_count)
         def _():
-            arriving = group_at(step + 1)
-            across(arriving).wait_recv()
-            pack(arriving)
-
-        work(group_at(step))
+            back(group).start()
+
         return carry
 
     lax.fori_loop(0, mem_count, step_work, 0)
-    out[0] = out[0] * scale
+    total = sums[0, 0]
+    for offset in range(1, mem_count):
+        back(jnp.int32(offset)).wait_recv()
+        total = total + sums[1, offset]
+    out[0] = total * scale
 
     for offset in range(1, mem_count):
         across(jnp.int32(offset)).wait_send()
-    for number, direction in enumerate(DIRECTIONS):
-
-        @pl.when(present(direction))
-        def _():
-            for copy in fixed_copies(number, direction):
-                copy.wait_send()
-            for group in range(mem_count):
-                pert_copy(jnp.int32(group), number, direction).wait_send()
+        back(jnp.int32(offset)).wait_send()
+    for_targets(lambda number, direction: coef_copy(number, direction).wait_send())
+    for group in range(mem_count):
+        for_targets(lambda number, direction: pert_copy(jnp.int32(group), number, direction).wait_send())
+        for_targets(lambda number, direction: grad_copy(jnp.int32(group), number, direction).wait_send())
 
 
 def body(mesh_sizes, gradient, perturbations, filter_coef):
@@ -343,17 +375,23 @@
             pltpu.VMEM((mem_count, 2, rows, LANES), jnp.bfloat16),
             pltpu.VMEM((mem_count, 2, packed, cols + 2 * LANES), jnp.bfloat16),
             pltpu.VMEM((mem_count, 2, rows, LANES), jnp.bfloat16),
-            pltpu.VMEM((6, rows + 2 * SUB, cols + 2 * LANES), jnp.float32),
+            pltpu.VMEM((5, rows + 2 * SUB, cols + 2 * LANES), jnp.float32),
             pltpu.VMEM((9, full_rows, full_cols), jnp.float32),
             pltpu.VMEM((2, full_rows, full_cols), jnp.float32),
+            pltpu.VMEM((mem_count, rows + 2 * SUB, cols + 2 * LANES), jnp.float32),
+            pltpu.VMEM((2, mem_count, rows, cols), jnp.float32),
             pltpu.SemaphoreType.DMA((mem_count,)),
             pltpu.SemaphoreType.DMA((mem_count,)),
-            pltpu.SemaphoreType.DMA((2 + mem_count, len(DIRECTIONS))),
-            pltpu.SemaphoreType.DMA((2 + mem_count, len(DIRECTIONS))),
-            pltpu.SemaphoreType.DMA((3,)),
+            pltpu.SemaphoreType.DMA((mem_count,)),
+            pltpu.SemaphoreType.DMA((mem_count,)),
+            pltpu.SemaphoreType.DMA((mem_count, len(DIRECTIONS))),
+            pltpu.SemaphoreType.DMA((mem_count, len(DIRECTIONS))),
+            pltpu.SemaphoreType.DMA((mem_count + 1, len(DIRECTIONS))),
+            pltpu.SemaphoreType.DMA((mem_count + 1, len(DIRECTIONS))),
+            pltpu.SemaphoreType.DMA((2 + mem_count,)),
         ],
         compiler_params=pltpu.CompilerParams(
-            collective_id=0, has_side_effects=True, vmem_limit_bytes=32 * 1024 * 1024
+            collective_id=0, has_side_effects=True, vmem_limit_bytes=60 * 1024 * 1024
         ),
     )(perturbations, gradient, filter_coef)
 

time: 25.6 us -> 25.1 us (0.980); the launches traced: 25.2 us -> 25 us
  local copies, waits for them, and re-layouts: 3.26 us -> 1.38 us
  Pallas kernels: 21.9 us -> 23.6 us
    unnamed x7 -> x1, local copies, waits for them, and re-layouts: 3.26 us -> 1.38 us
    pallas_call x1, Pallas kernels: 21.9 us -> 23.6 us  [body(): pl.pallas_call(functools.partial(kernel, sizes), out_shape=jax.ShapeDtype...]
where the time goes in v3:
time: 25.1 us; the launch traced here: 25 us
  Pallas kernels  23.6 us (94%)
  local copies, waits for them, and re-layouts  1.38 us (5%)
    pallas_call x1, Pallas kernels, body(): pl.pallas_call(functools.partial(kernel, sizes), out_shape=jax.ShapeDtype...  23.6 us
    unnamed x1, local copies, waits for them, and re-layouts  1.38 us

profile of v3, /device:TPU:0, one launch (start us, length us, event | category | flops | bytes accessed | tf_op | source)
XLA Modules:
  0.0 25.0 jit_solution(13229342776559240876)
XLA Ops:
  0.0 23.6 %shard_map.37 = f32[1,32,256]{2,1,0:T(8,128)} custom-call(bf16[5,4,32,256]{3,2,1,0:T(8,128)(2,1)} %pert.1, f32[1,32,256]{2,1,0:T(8,128)} %grad.1, f32[5,32,256]{2,1,0:T(8,128)} %coef.1), custom_call_target="tpu_custom_call" | custom-call | tf_op jit(solution)/shard_map/pallas_call | solution.py:366
  23.6 1.4 %copy.5 = f32[1,32,256]{2,1,0:T(8,128)} copy(f32[1,32,256]{2,1,0:T(8,128)} %shard_map.37) | data formatting | bytes 65536

commit v4 on v3

--- a/solution.py
+++ b/solution.py
@@ -14,7 +14,38 @@
 
 
 def shifted(values, offset, axis):
-    return pltpu.roll(values, (-offset) % values.shape[axis], axis)
+    unit = (SUB, LANES)[axis]
+    size = values.shape[axis]
+    if offset < 0:
+        edge = pltpu.roll(lax.slice_in_dim(values, size - unit, size, axis=axis), 1, axis)
+        return jnp.concatenate([edge, lax.slice_in_dim(values, 0, size - unit, axis=axis)], axis=axis)
+    edge = pltpu.roll(lax.slice_in_dim(values, 0, unit, axis=axis), unit - 1, axis)
+    return jnp.concatenate([lax.slice_in_dim(values, unit, size, axis=axis), edge], axis=axis)
+
+
+def place_of(index, unit, size):
+    return (index % unit) * (size // unit) + index // unit
+
+
+def ones_where(condition):
+    return jnp.where(condition, 1.0, 0.0).astype(jnp.bfloat16)
+
+
+def iotas(shape):
+    return [lax.broadcasted_iota(jnp.int32, shape, axis) for axis in range(2)]
+
+
+def parts_of(values):
+    high = values.astype(jnp.bfloat16).astype(jnp.float32)
+    rest = values - high
+    middle = rest.astype(jnp.bfloat16).astype(jnp.float32)
+    return jnp.concatenate(
+        [high, middle, rest - middle, jnp.zeros((SUB, values.shape[1]), jnp.float32)], axis=0
+    ).astype(jnp.bfloat16)
+
+
+def product(left, right):
+    return jnp.dot(left, right, preferred_element_type=jnp.float32)
 
 
 def circular(centre_rows, north_rows, south_rows, row_low):
@@ -44,6 +75,11 @@
     scaled,
     grads,
     sums,
+    perm_cols,
+    perm_rows,
+    perm_parts,
+    back_cols,
+    back_parts,
     z_send,
     z_recv,
     sum_send,
@@ -249,19 +285,45 @@
     for_sources(lambda number, direction: coef_copy(number, direction).wait_recv())
 
     full_rows, full_cols = rows + 2 * HALO, cols + LANES
-    row_index = lax.broadcasted_iota(jnp.int32, (full_rows, full_cols), 0)
-    col_index = lax.broadcasted_iota(jnp.int32, (full_rows, full_cols), 1)
-    row_index = jnp.where(row_index < rows + HALO, row_index, row_index - full_rows)
-    col_index = jnp.where(col_index < cols + LANES // 2, col_index, col_index - full_cols)
-    near = (col_index >= -HALO) & (col_index < cols + HALO)
-    row_index = row_index + lat * rows
-    col_index = col_index + lon * cols
-    inside = (
-        near
-        & (row_index >= 0)
-        & (row_index < rows * lat_count)
-        & (col_index >= 0)
-        & (col_index < cols * lon_count)
+
+    def inside_of(row_index, col_index):
+        row_index = jnp.where(row_index < rows + HALO, row_index, row_index - full_rows)
+        col_index = jnp.where(col_index < cols + LANES // 2, col_index, col_index - full_cols)
+        near = (col_index >= -HALO) & (col_index < cols + HALO)
+        row_index = row_index + lat * rows
+        col_index = col_index + lon * cols
+        return (
+            near
+            & (row_index >= 0)
+            & (row_index < rows * lat_count)
+            & (col_index >= 0)
+            & (col_index < cols * lon_count)
+        )
+
+    row_index, col_index = iotas((full_rows, full_cols))
+    inside = inside_of(row_index, col_index)
+    inside_here = inside_of(
+        place_of(row_index, SUB, full_rows), place_of(col_index, LANES, full_cols)
+    )
+    scaled[1] = inside.astype(jnp.float32)
+
+    source, target = iotas((full_cols, full_cols))
+    perm_cols[...] = ones_where(source == place_of(target, LANES, full_cols))
+    source, target = iotas((full_cols, cols))
+    back_cols[...] = ones_where(target == place_of(source, LANES, full_cols))
+    target, source = iotas(perm_rows.shape)
+    perm_rows[...] = ones_where(
+        source == target // full_rows * full_rows + place_of(target % full_rows, SUB, full_rows)
+    )
+    target, source = iotas(perm_parts.shape)
+    perm_parts[...] = ones_where(
+        (source < 3 * full_rows)
+        & (source % full_rows == place_of(target, SUB, full_rows))
+    )
+    target, source = iotas(back_parts.shape)
+    back_parts[...] = ones_where(
+        (source < 3 * full_rows)
+        & (target == place_of(source % full_rows, SUB, full_rows))
     )
     low_row_full = lax.broadcasted_iota(jnp.int32, (SUB, full_cols), 0) < HALO
 
@@ -270,7 +332,9 @@
         wide = circular(
             wide[SUB : SUB + rows], wide[:SUB], wide[SUB + rows :], low_row_full
         )
-        return jnp.where(inside, wide, 0.0)
+        wide = parts_of(jnp.where(scaled[1] > 0.5, wide, 0.0))
+        wide = product(wide, perm_cols[...]).astype(jnp.bfloat16)
+        return product(perm_parts[...], wide)
 
     c0, cn, cs, cw, ce = (extended(ext[index]) for index in range(5))
     for index, value in enumerate((c0, cn, cs, cw, ce)):
@@ -278,8 +342,7 @@
     for index, value in enumerate(
         (shifted(cs, -1, 0), shifted(cn, 1, 0), shifted(ce, -1, 1), shifted(cw, 1, 1))
     ):
-        stencils[5 + index] = jnp.where(inside, value, 0.0)
-    scaled[1] = inside.astype(jnp.float32)
+        stencils[5 + index] = jnp.where(inside_here, value, 0.0)
 
     def one_pass(values, first):
         total = stencils[0] * values + stencils[first] * shifted(values, -1, 0)
@@ -291,11 +354,12 @@
         for_sources(lambda number, direction: pert_copy(group, number, direction).wait_recv())
         for_sources(lambda number, direction: grad_copy(group, number, direction).wait_recv())
         scaled[0] = extended(grads[group])
-        total = jnp.zeros((rows, cols), jnp.float32)
+        total = jnp.zeros((full_rows, full_cols), jnp.float32)
         south = folded(recv_rows[group, 0].astype(jnp.float32), cols)
         north = folded(recv_rows[group, 1].astype(jnp.float32), cols)
         from_east = recv_cols[group, 0].astype(jnp.float32)
         from_west = recv_cols[group, 1].astype(jnp.float32)
+        blocks = []
         for k in range(per_mem):
             block = centre[group, k].astype(jnp.float32)
             tile = slice((k // 2) * SUB, (k // 2 + 1) * SUB)
@@ -306,17 +370,26 @@
             east = pltpu.roll(from_east, LANES - HALO * k, 1) if k else from_east
             west = pltpu.roll(from_west, (-HALO * (k + 1)) % LANES, 1)
             side = jnp.where(lane < LANES // 2, east, west)
-            field[k] = circular(
+            block = circular(
                 jnp.concatenate([block, side], axis=1), north_rows, south_rows, low_row_full
             )
+            blocks.append(jnp.where(scaled[1] > 0.5, block, 0.0))
+        missing = perm_rows.shape[1] - per_mem * full_rows
+        if missing:
+            blocks.append(jnp.zeros((missing, full_cols), jnp.float32))
+        stack = jnp.concatenate(blocks, axis=0).astype(jnp.bfloat16)
+        stack = product(stack, perm_cols[...]).astype(jnp.bfloat16)
+        field[...] = product(perm_rows[...], stack)
         for k in range(per_mem):
-            values = jnp.where(scaled[1] > 0.5, field[k] * scaled[0], 0.0)
+            here = slice(k * full_rows, (k + 1) * full_rows)
+            values = field[here] * scaled[0]
             values = one_pass(values, 5)
             values = one_pass(values, 5)
             values = one_pass(values, 1)
             values = one_pass(values, 1)
-            total = total + values[:rows, :cols] * field[k, :rows, :cols]
-        sums[0, group] = total
+            total = total + values * field[here]
+        total = product(parts_of(total), back_cols[...]).astype(jnp.bfloat16)
+        sums[0, group] = product(back_parts[...], total)
 
     if mem_count > 1:
         across(jnp.int32(1)).wait_recv()
@@ -370,7 +443,7 @@
         out_specs=pl.BlockSpec(memory_space=pltpu.VMEM),
         scratch_shapes=[
             pltpu.VMEM((mem_count, per_mem, rows, cols), jnp.bfloat16),
-            pltpu.VMEM((per_mem, full_rows, full_cols), jnp.float32),
+            pltpu.VMEM((per_mem * full_rows, full_cols), jnp.float32),
             pltpu.VMEM((mem_count, 2, packed, cols), jnp.bfloat16),
             pltpu.VMEM((mem_count, 2, rows, LANES), jnp.bfloat16),
             pltpu.VMEM((mem_count, 2, packed, cols + 2 * LANES), jnp.bfloat16),
@@ -380,6 +453,11 @@
             pltpu.VMEM((2, full_rows, full_cols), jnp.float32),
             pltpu.VMEM((mem_count, rows + 2 * SUB, cols + 2 * LANES), jnp.float32),
             pltpu.VMEM((2, mem_count, rows, cols), jnp.float32),
+            pltpu.VMEM((full_cols, full_cols), jnp.bfloat16),
+            pltpu.VMEM((per_mem * full_rows, -(-per_mem * full_rows // 16) * 16), jnp.bfloat16),
+            pltpu.VMEM((full_rows, 3 * full_rows + SUB), jnp.bfloat16),
+            pltpu.VMEM((full_cols, cols), jnp.bfloat16),
+            pltpu.VMEM((rows, 3 * full_rows + SUB), jnp.bfloat16),
             pltpu.SemaphoreType.DMA((mem_count,)),
             pltpu.SemaphoreType.DMA((mem_count,)),
             pltpu.SemaphoreType.DMA((mem_count,)),

time: 25.1 us -> 26.3 us (1.048)
  Pallas kernels: 23.6 us -> 24.7 us
    pallas_call x1, Pallas kernels: 23.6 us -> 24.7 us  [body(): pl.pallas_call(functools.partial(kernel, sizes), out_shape=jax.ShapeDtype...]
where the time goes in v4:
time: 26.3 us; the launch traced here: 26.1 us
  Pallas kernels  24.7 us (94%)
  local copies, waits for them, and re-layouts  1.38 us (5%)
    pallas_call x1, Pallas kernels, body(): pl.pallas_call(functools.partial(kernel, sizes), out_shape=jax.ShapeDtype...  24.7 us
    unnamed x1, local copies, waits for them, and re-layouts  1.38 us

profile of v4, /device:TPU:0, one launch (start us, length us, event | category | flops | bytes accessed | tf_op | source)
XLA Modules:
  0.0 26.1 jit_solution(8205026461425283694)
XLA Ops:
  0.0 24.7 %shard_map.37 = f32[1,32,256]{2,1,0:T(8,128)} custom-call(bf16[5,4,32,256]{3,2,1,0:T(8,128)(2,1)} %pert.1, f32[1,32,256]{2,1,0:T(8,128)} %grad.1, f32[5,32,256]{2,1,0:T(8,128)} %coef.1), custom_call_target="tpu_custom_call" | custom-call | tf_op jit(solution)/shard_map/pallas_call | solution.py:439
  24.7 1.4 %copy.5 = f32[1,32,256]{2,1,0:T(8,128)} copy(f32[1,32,256]{2,1,0:T(8,128)} %shard_map.37) | data formatting | bytes 65536

commit v5 on v4

--- a/solution.py
+++ b/solution.py
@@ -84,8 +84,6 @@
     z_recv,
     sum_send,
     sum_recv,
-    grad_send,
-    grad_recv,
     halo_send,
     halo_recv,
     local_sem,
@@ -128,19 +126,61 @@
 
     inner_rows, inner_cols = pl.ds(SUB, rows), pl.ds(LANES, cols)
 
-    def own_pert(group):
-        return pltpu.make_async_copy(pert.at[:, peer(group)], centre.at[group], local_sem.at[2 + group])
-
+    own_pert = pltpu.make_async_copy(pert, centre, local_sem.at[2])
     own_grad = pltpu.make_async_copy(
         grad.at[0], grads.at[0, inner_rows, inner_cols], local_sem.at[0]
     )
     own_coef = pltpu.make_async_copy(
         coef, ext.at[:, inner_rows, inner_cols], local_sem.at[1]
     )
-    for step in range(mem_count):
-        own_pert(group_at(jnp.int32(step))).start()
+    own_pert.start()
     own_grad.start()
     own_coef.start()
+
+    full_rows, full_cols = rows + 2 * HALO, cols + LANES
+
+    def inside_of(row_index, col_index):
+        row_index = jnp.where(row_index < rows + HALO, row_index, row_index - full_rows)
+        col_index = jnp.where(col_index < cols + LANES // 2, col_index, col_index - full_cols)
+        near = (col_index >= -HALO) & (col_index < cols + HALO)
+        row_index = row_index + lat * rows
+        col_index = col_index + lon * cols
+        return (
+            near
+            & (row_index >= 0)
+            & (row_index < rows * lat_count)
+            & (col_index >= 0)
+            & (col_index < cols * lon_count)
+        )
+
+    def line(size, axis):
+        return lax.broadcasted_iota(jnp.int32, (size, 1) if axis == 0 else (1, size), axis)
+
+    inside = inside_of(*iotas((full_rows, full_cols)))
+    scaled[1] = inside.astype(jnp.float32)
+    inside_here = inside_of(
+        place_of(line(full_rows, 0), SUB, full_rows), place_of(line(full_cols, 1), LANES, full_cols)
+    )
+
+    def sized(ref, axis):
+        return line(ref.shape[axis], axis)
+
+    place = place_of(sized(perm_cols, 1), LANES, full_cols)
+    perm_cols[...] = ones_where(iotas(perm_cols.shape)[0] == place)
+    place = place_of(sized(back_cols, 0), LANES, full_cols)
+    back_cols[...] = ones_where(iotas(back_cols.shape)[1] == place)
+    target = sized(perm_rows, 0)
+    place = target // full_rows * full_rows + place_of(target % full_rows, SUB, full_rows)
+    perm_rows[...] = ones_where(iotas(perm_rows.shape)[1] == place)
+    source = sized(perm_parts, 1)
+    source = jnp.where(source < 3 * full_rows, source % full_rows, -1)
+    place = place_of(sized(perm_parts, 0), SUB, full_rows)
+    perm_parts[...] = ones_where(source == place)
+    source = sized(back_parts, 1)
+    place = place_of(source % full_rows, SUB, full_rows)
+    place = jnp.where(source < 3 * full_rows, place, -1)
+    back_parts[...] = ones_where(iotas(back_parts.shape)[0] == place)
+    low_row_full = lax.broadcasted_iota(jnp.int32, (SUB, full_cols), 0) < HALO
 
     blocks = [
         1 + jnp.where(here > 0, 1, 0) + jnp.where(here < count - 1, 1, 0)
@@ -184,22 +224,41 @@
         return pltpu.make_async_remote_copy(
             src_ref=coef.at[:, source_rows, source_cols],
             dst_ref=ext.at[:, target_rows, target_cols],
-            send_sem=halo_send.at[mem_count, number],
-            recv_sem=halo_recv.at[mem_count, number],
+            send_sem=halo_send.at[0, number],
+            recv_sem=halo_recv.at[0, number],
             device_id=neighbour(direction),
             device_id_type=mesh_id,
         )
 
-    def grad_copy(group, number, direction):
+    def grad_copy(number, direction):
         source_rows, target_rows = span(direction[0], SUB, rows, SUB)
         source_cols, target_cols = span(direction[1], LANES, cols, LANES)
         source_rows = pl.ds(source_rows.start + SUB, source_rows.size)
         source_cols = pl.ds(source_cols.start + LANES, source_cols.size)
         return pltpu.make_async_remote_copy(
-            src_ref=grads.at[group, source_rows, source_cols],
-            dst_ref=grads.at[group, target_rows, target_cols],
-            send_sem=grad_send.at[group, number],
-            recv_sem=grad_recv.at[group, number],
+            src_ref=grads.at[:, source_rows, source_cols],
+            dst_ref=grads.at[:, target_rows, target_cols],
+            send_sem=halo_send.at[1, number],
+            recv_sem=halo_recv.at[1, number],
+            device_id=neighbour(direction),
+            device_id_type=mesh_id,
+        )
+
+    def pert_copy(number, direction):
+        up, right = direction
+        if up == 0:
+            side = 0 if right < 0 else 1
+            source, target = send_cols.at[side], recv_cols.at[side]
+        else:
+            side = 0 if up < 0 else 1
+            source_cols, target_cols = span(right, LANES, cols, LANES)
+            source = send_rows.at[side, :, :, source_cols]
+            target = recv_rows.at[side, :, :, target_cols]
+        return pltpu.make_async_remote_copy(
+            src_ref=source,
+            dst_ref=target,
+            send_sem=halo_send.at[2, number],
+            recv_sem=halo_recv.at[2, number],
             device_id=neighbour(direction),
             device_id_type=mesh_id,
         )
@@ -218,36 +277,17 @@
             def _():
                 action(number, direction)
 
-    def pert_copy(group, number, direction):
-        up, right = direction
-        if up == 0:
-            side = 0 if right < 0 else 1
-            source, target = send_cols.at[group, side], recv_cols.at[group, side]
-        else:
-            side = 0 if up < 0 else 1
-            source_cols, target_cols = span(right, LANES, cols, LANES)
-            source = send_rows.at[group, side, :, source_cols]
-            target = recv_rows.at[group, side, :, target_cols]
-        return pltpu.make_async_remote_copy(
-            src_ref=source,
-            dst_ref=target,
-            send_sem=halo_send.at[group, number],
-            recv_sem=halo_recv.at[group, number],
-            device_id=neighbour(direction),
-            device_id_type=mesh_id,
-        )
-
     for_targets(lambda number, direction: coef_copy(number, direction).start())
 
     low_row = lax.broadcasted_iota(jnp.int32, (SUB, cols), 0) < HALO
     lane = lax.broadcasted_iota(jnp.int32, (rows, LANES), 1)
     tiles = send_rows.shape[2] // SUB
 
-    def pack(group):
+    def pack(group, carry):
         tops, bottoms = [], []
         west = east = None
         for k in range(per_mem):
-            block = centre[group, k].astype(jnp.float32)
+            block = centre[k, peer(group)].astype(jnp.float32)
             top, bottom = block[:SUB], block[rows - SUB :]
             if k % 2:
                 tops[-1] = jnp.where(low_row, tops[-1], pltpu.roll(top, HALO, 0))
@@ -263,69 +303,17 @@
         while len(tops) < tiles:
             tops.append(tops[-1])
             bottoms.append(bottoms[-1])
-        send_rows[group, 0] = jnp.concatenate(tops, axis=0).astype(jnp.bfloat16)
-        send_rows[group, 1] = jnp.concatenate(bottoms, axis=0).astype(jnp.bfloat16)
-        send_cols[group, 0] = west.astype(jnp.bfloat16)
-        send_cols[group, 1] = east.astype(jnp.bfloat16)
-        for_targets(lambda number, direction: pert_copy(group, number, direction).start())
-
-    def forward(group):
-        for_targets(lambda number, direction: grad_copy(group, number, direction).start())
-
-    def pack_step(step, carry):
-        group = group_at(step)
-        own_pert(group).wait()
-        pack(group)
+        send_rows[0, group] = jnp.concatenate(tops, axis=0).astype(jnp.bfloat16)
+        send_rows[1, group] = jnp.concatenate(bottoms, axis=0).astype(jnp.bfloat16)
+        send_cols[0, group] = west.astype(jnp.bfloat16)
+        send_cols[1, group] = east.astype(jnp.bfloat16)
         return carry
 
-    lax.fori_loop(0, mem_count, pack_step, 0)
-    own_grad.wait()
-    forward(jnp.int32(0))
+    own_pert.wait()
+    lax.fori_loop(0, mem_count, pack, 0)
+    for_targets(lambda number, direction: pert_copy(number, direction).start())
     own_coef.wait()
     for_sources(lambda number, direction: coef_copy(number, direction).wait_recv())
-
-    full_rows, full_cols = rows + 2 * HALO, cols + LANES
-
-    def inside_of(row_index, col_index):
-        row_index = jnp.where(row_index < rows + HALO, row_index, row_index - full_rows)
-        col_index = jnp.where(col_index < cols + LANES // 2, col_index, col_index - full_cols)
-        near = (col_index >= -HALO) & (col_index < cols + HALO)
-        row_index = row_index + lat * rows
-        col_index = col_index + lon * cols
-        return (
-            near
-            & (row_index >= 0)
-            & (row_index < rows * lat_count)
-            & (col_index >= 0)
-            & (col_index < cols * lon_count)
-        )
-
-    row_index, col_index = iotas((full_rows, full_cols))
-    inside = inside_of(row_index, col_index)
-    inside_here = inside_of(
-        place_of(row_index, SUB, full_rows), place_of(col_index, LANES, full_cols)
-    )
-    scaled[1] = inside.astype(jnp.float32)
-
-    source, target = iotas((full_cols, full_cols))
-    perm_cols[...] = ones_where(source == place_of(target, LANES, full_cols))
-    source, target = iotas((full_cols, cols))
-    back_cols[...] = ones_where(target == place_of(source, LANES, full_cols))
-    target, source = iotas(perm_rows.shape)
-    perm_rows[...] = ones_where(
-        source == target // full_rows * full_rows + place_of(target % full_rows, SUB, full_rows)
-    )
-    target, source = iotas(perm_parts.shape)
-    perm_parts[...] = ones_where(
-        (source < 3 * full_rows)
-        & (source % full_rows == place_of(target, SUB, full_rows))
-    )
-    target, source = iotas(back_parts.shape)
-    back_parts[...] = ones_where(
-        (source < 3 * full_rows)
-        & (target == place_of(source % full_rows, SUB, full_rows))
-    )
-    low_row_full = lax.broadcasted_iota(jnp.int32, (SUB, full_cols), 0) < HALO
 
     def extended(block):
         wide = folded(block, cols)
@@ -350,18 +338,20 @@
         total = total + stencils[first + 2] * shifted(values, -1, 1)
         return total + stencils[first + 3] * shifted(values, 1, 1)
 
-    def work(group):
-        for_sources(lambda number, direction: pert_copy(group, number, direction).wait_recv())
-        for_sources(lambda number, direction: grad_copy(group, number, direction).wait_recv())
-        scaled[0] = extended(grads[group])
-        total = jnp.zeros((full_rows, full_cols), jnp.float32)
-        south = folded(recv_rows[group, 0].astype(jnp.float32), cols)
-        north = folded(recv_rows[group, 1].astype(jnp.float32), cols)
-        from_east = recv_cols[group, 0].astype(jnp.float32)
-        from_west = recv_cols[group, 1].astype(jnp.float32)
+    own_grad.wait()
+    for offset in range(1, mem_count):
+        across(jnp.int32(offset)).wait_recv()
+    for_targets(lambda number, direction: grad_copy(number, direction).start())
+    for_sources(lambda number, direction: pert_copy(number, direction).wait_recv())
+
+    def build(group, carry):
+        south = folded(recv_rows[0, group].astype(jnp.float32), cols)
+        north = folded(recv_rows[1, group].astype(jnp.float32), cols)
+        from_east = recv_cols[0, group].astype(jnp.float32)
+        from_west = recv_cols[1, group].astype(jnp.float32)
         blocks = []
         for k in range(per_mem):
-            block = centre[group, k].astype(jnp.float32)
+            block = centre[k, peer(group)].astype(jnp.float32)
             tile = slice((k // 2) * SUB, (k // 2 + 1) * SUB)
             south_rows, north_rows = south[tile], north[tile]
             if k % 2:
@@ -379,30 +369,26 @@
             blocks.append(jnp.zeros((missing, full_cols), jnp.float32))
         stack = jnp.concatenate(blocks, axis=0).astype(jnp.bfloat16)
         stack = product(stack, perm_cols[...]).astype(jnp.bfloat16)
-        field[...] = product(perm_rows[...], stack)
+        field[group] = product(perm_rows[...], stack)
+        return carry
+
+    lax.fori_loop(0, mem_count, build, 0)
+    for_sources(lambda number, direction: grad_copy(number, direction).wait_recv())
+
+    def step_work(step, carry):
+        group = group_at(step)
+        scaled[0] = extended(grads[group])
+        total = jnp.zeros((full_rows, full_cols), jnp.float32)
         for k in range(per_mem):
             here = slice(k * full_rows, (k + 1) * full_rows)
-            values = field[here] * scaled[0]
+            values = field[group, here] * scaled[0]
             values = one_pass(values, 5)
             values = one_pass(values, 5)
             values = one_pass(values, 1)
             values = one_pass(values, 1)
-            total = total + values * field[here]
+            total = total + values * field[group, here]
         total = product(parts_of(total), back_cols[...]).astype(jnp.bfloat16)
         sums[0, group] = product(back_parts[...], total)
-
-    if mem_count > 1:
-        across(jnp.int32(1)).wait_recv()
-        forward(jnp.int32(1))
-
-    def step_work(step, carry):
-        @pl.when(step + 2 < mem_count)
-        def _():
-            across(step + 2).wait_recv()
-            forward(step + 2)
-
-        group = group_at(step)
-        work(group)
 
         @pl.when(step + 1 < mem_count)
         def _():
@@ -420,10 +406,12 @@
     for offset in range(1, mem_count):
         across(jnp.int32(offset)).wait_send()
         back(jnp.int32(offset)).wait_send()
-    for_targets(lambda number, direction: coef_copy(number, direction).wait_send())
-    for group in range(mem_count):
-        for_targets(lambda number, direction: pert_copy(jnp.int32(group), number, direction).wait_send())
-        for_targets(lambda number, direction: grad_copy(jnp.int32(group), number, direction).wait_send())
+
+    def sent(number, direction):
+        for copy in (coef_copy, grad_copy, pert_copy):
+            copy(number, direction).wait_send()
+
+    for_targets(sent)
 
 
 def body(mesh_sizes, gradient, perturbations, filter_coef):
@@ -442,12 +430,12 @@
         in_specs=[pl.BlockSpec(memory_space=pltpu.HBM)] * 3,
         out_specs=pl.BlockSpec(memory_space=pltpu.VMEM),
         scratch_shapes=[
-            pltpu.VMEM((mem_count, per_mem, rows, cols), jnp.bfloat16),
-            pltpu.VMEM((per_mem * full_rows, full_cols), jnp.float32),
-            pltpu.VMEM((mem_count, 2, packed, cols), jnp.bfloat16),
-            pltpu.VMEM((mem_count, 2, rows, LANES), jnp.bfloat16),
-            pltpu.VMEM((mem_count, 2, packed, cols + 2 * LANES), jnp.bfloat16),
-            pltpu.VMEM((mem_count, 2, rows, LANES), jnp.bfloat16),
+            pltpu.VMEM((per_mem, mem_count, rows, cols), jnp.bfloat16),
+            pltpu.VMEM((mem_count, per_mem * full_rows, full_cols), jnp.float32),
+            pltpu.VMEM((2, mem_count, packed, cols), jnp.bfloat16),
+            pltpu.VMEM((2, mem_count, rows, LANES), jnp.bfloat16),
+            pltpu.VMEM((2, mem_count, packed, cols + 2 * LANES), jnp.bfloat16),
+            pltpu.VMEM((2, mem_count, rows, LANES), jnp.bfloat16),
             pltpu.VMEM((5, rows + 2 * SUB, cols + 2 * LANES), jnp.float32),
             pltpu.VMEM((9, full_rows, full_cols), jnp.float32),
             pltpu.VMEM((2, full_rows, full_cols), jnp.float32),
@@ -462,11 +450,9 @@
             pltpu.SemaphoreType.DMA((mem_count,)),
             pltpu.SemaphoreType.DMA((mem_count,)),
             pltpu.SemaphoreType.DMA((mem_count,)),
-            pltpu.SemaphoreType.DMA((mem_count, len(DIRECTIONS))),
-            pltpu.SemaphoreType.DMA((mem_count, len(DIRECTIONS))),
-            pltpu.SemaphoreType.DMA((mem_count + 1, len(DIRECTIONS))),
-            pltpu.SemaphoreType.DMA((mem_count + 1, len(DIRECTIONS))),
-            pltpu.SemaphoreType.DMA((2 + mem_count,)),
+            pltpu.SemaphoreType.DMA((3, len(DIRECTIONS))),
+            pltpu.SemaphoreType.DMA((3, len(DIRECTIONS))),
+            pltpu.SemaphoreType.DMA((3,)),
         ],
         compiler_params=pltpu.CompilerParams(
             collective_id=0, has_side_effects=True, vmem_limit_bytes=60 * 1024 * 1024

time: 26.3 us -> 23.6 us (0.90)
  Pallas kernels: 24.7 us -> 22.1 us
    pallas_call x1, Pallas kernels: 24.7 us -> 22.1 us  [body(): pl.pallas_call(functools.partial(kernel, sizes), out_shape=jax.ShapeDtype...]
where the time goes in v5:
time: 23.6 us; the launch traced here: 23.5 us
  Pallas kernels  22.1 us (94%)
  local copies, waits for them, and re-layouts  1.38 us (6%)
    pallas_call x1, Pallas kernels, body(): pl.pallas_call(functools.partial(kernel, sizes), out_shape=jax.ShapeDtype...  22.1 us
    unnamed x1, local copies, waits for them, and re-layouts  1.38 us

profile of v5, /device:TPU:0, one launch (start us, length us, event | category | flops | bytes accessed | tf_op | source)
XLA Modules:
  0.0 23.5 jit_solution(13681001376673021569)
XLA Ops:
  0.0 22.1 %shard_map.37 = f32[1,32,256]{2,1,0:T(8,128)} custom-call(bf16[5,4,32,256]{3,2,1,0:T(8,128)(2,1)} %pert.1, f32[1,32,256]{2,1,0:T(8,128)} %grad.1, f32[5,32,256]{2,1,0:T(8,128)} %coef.1), custom_call_target="tpu_custom_call" | custom-call | tf_op jit(solution)/shard_map/pallas_call | solution.py:427
  22.1 1.4 %copy.5 = f32[1,32,256]{2,1,0:T(8,128)} copy(f32[1,32,256]{2,1,0:T(8,128)} %shard_map.37) | data formatting | bytes 65536

commit v6 on v5

--- a/solution.py
+++ b/solution.py
@@ -14,38 +14,37 @@
 
 
 def shifted(values, offset, axis):
-    unit = (SUB, LANES)[axis]
     size = values.shape[axis]
+    if axis == 1:
+        return pltpu.roll(values, (-offset) % size, 1)
     if offset < 0:
-        edge = pltpu.roll(lax.slice_in_dim(values, size - unit, size, axis=axis), 1, axis)
-        return jnp.concatenate([edge, lax.slice_in_dim(values, 0, size - unit, axis=axis)], axis=axis)
-    edge = pltpu.roll(lax.slice_in_dim(values, 0, unit, axis=axis), unit - 1, axis)
-    return jnp.concatenate([lax.slice_in_dim(values, unit, size, axis=axis), edge], axis=axis)
+        edge = pltpu.roll(values[size - SUB :], 1, 0)
+        return jnp.concatenate([edge, values[: size - SUB]], axis=0)
+    edge = pltpu.roll(values[:SUB], SUB - 1, 0)
+    return jnp.concatenate([values[SUB:], edge], axis=0)
 
 
 def place_of(index, unit, size):
     return (index % unit) * (size // unit) + index // unit
 
 
-def ones_where(condition):
-    return jnp.where(condition, 1.0, 0.0).astype(jnp.bfloat16)
-
-
-def iotas(shape):
-    return [lax.broadcasted_iota(jnp.int32, shape, axis) for axis in range(2)]
-
-
-def parts_of(values):
-    high = values.astype(jnp.bfloat16).astype(jnp.float32)
-    rest = values - high
-    middle = rest.astype(jnp.bfloat16).astype(jnp.float32)
+def columns_of(values):
+    return [values[:, low : low + LANES] for low in range(0, values.shape[1], LANES)]
+
+
+def interleaved(ref, values):
+    tiles = values.shape[0] // SUB
+    for u, column in enumerate(columns_of(values)):
+        ref[u] = column
     return jnp.concatenate(
-        [high, middle, rest - middle, jnp.zeros((SUB, values.shape[1]), jnp.float32)], axis=0
-    ).astype(jnp.bfloat16)
-
-
-def product(left, right):
-    return jnp.dot(left, right, preferred_element_type=jnp.float32)
+        [
+            jnp.concatenate(
+                [ref[u, pl.ds(t, SUB, stride=tiles), :] for t in range(tiles)], axis=0
+            )
+            for u in range(ref.shape[0])
+        ],
+        axis=1,
+    )
 
 
 def circular(centre_rows, north_rows, south_rows, row_low):
@@ -75,11 +74,8 @@
     scaled,
     grads,
     sums,
-    perm_cols,
-    perm_rows,
-    perm_parts,
-    back_cols,
-    back_parts,
+    wide_sums,
+    natural,
     z_send,
     z_recv,
     sum_send,
@@ -153,33 +149,12 @@
             & (col_index < cols * lon_count)
         )
 
-    def line(size, axis):
-        return lax.broadcasted_iota(jnp.int32, (size, 1) if axis == 0 else (1, size), axis)
-
-    inside = inside_of(*iotas((full_rows, full_cols)))
+    row_index, col_index = (
+        lax.broadcasted_iota(jnp.int32, (full_rows, full_cols), axis) for axis in range(2)
+    )
+    inside = inside_of(row_index, col_index)
     scaled[1] = inside.astype(jnp.float32)
-    inside_here = inside_of(
-        place_of(line(full_rows, 0), SUB, full_rows), place_of(line(full_cols, 1), LANES, full_cols)
-    )
-
-    def sized(ref, axis):
-        return line(ref.shape[axis], axis)
-
-    place = place_of(sized(perm_cols, 1), LANES, full_cols)
-    perm_cols[...] = ones_where(iotas(perm_cols.shape)[0] == place)
-    place = place_of(sized(back_cols, 0), LANES, full_cols)
-    back_cols[...] = ones_where(iotas(back_cols.shape)[1] == place)
-    target = sized(perm_rows, 0)
-    place = target // full_rows * full_rows + place_of(target % full_rows, SUB, full_rows)
-    perm_rows[...] = ones_where(iotas(perm_rows.shape)[1] == place)
-    source = sized(perm_parts, 1)
-    source = jnp.where(source < 3 * full_rows, source % full_rows, -1)
-    place = place_of(sized(perm_parts, 0), SUB, full_rows)
-    perm_parts[...] = ones_where(source == place)
-    source = sized(back_parts, 1)
-    place = place_of(source % full_rows, SUB, full_rows)
-    place = jnp.where(source < 3 * full_rows, place, -1)
-    back_parts[...] = ones_where(iotas(back_parts.shape)[0] == place)
+    inside_here = inside_of(place_of(row_index, SUB, full_rows), col_index)
     low_row_full = lax.broadcasted_iota(jnp.int32, (SUB, full_cols), 0) < HALO
 
     blocks = [
@@ -200,8 +175,8 @@
 
     def back(offset):
         return pltpu.make_async_remote_copy(
-            src_ref=sums.at[0, offset],
-            dst_ref=sums.at[1, offset],
+            src_ref=wide_sums.at[offset, :, pl.ds(0, rows)],
+            dst_ref=sums.at[offset],
             send_sem=sum_send.at[offset],
             recv_sem=sum_recv.at[offset],
             device_id=(peer(offset), lat, lon),
@@ -315,16 +290,14 @@
     own_coef.wait()
     for_sources(lambda number, direction: coef_copy(number, direction).wait_recv())
 
-    def extended(block):
+    def extended(block, slot):
         wide = folded(block, cols)
         wide = circular(
             wide[SUB : SUB + rows], wide[:SUB], wide[SUB + rows :], low_row_full
         )
-        wide = parts_of(jnp.where(scaled[1] > 0.5, wide, 0.0))
-        wide = product(wide, perm_cols[...]).astype(jnp.bfloat16)
-        return product(perm_parts[...], wide)
-
-    c0, cn, cs, cw, ce = (extended(ext[index]) for index in range(5))
+        return interleaved(natural.at[slot], jnp.where(scaled[1] > 0.5, wide, 0.0))
+
+    c0, cn, cs, cw, ce = (extended(ext[index], index) for index in range(5))
     for index, value in enumerate((c0, cn, cs, cw, ce)):
         stencils[index] = value
     for index, value in enumerate(
@@ -349,7 +322,6 @@
         north = folded(recv_rows[1, group].astype(jnp.float32), cols)
         from_east = recv_cols[0, group].astype(jnp.float32)
         from_west = recv_cols[1, group].astype(jnp.float32)
-        blocks = []
         for k in range(per_mem):
             block = centre[k, peer(group)].astype(jnp.float32)
             tile = slice((k // 2) * SUB, (k // 2 + 1) * SUB)
@@ -363,13 +335,8 @@
             block = circular(
                 jnp.concatenate([block, side], axis=1), north_rows, south_rows, low_row_full
             )
-            blocks.append(jnp.where(scaled[1] > 0.5, block, 0.0))
-        missing = perm_rows.shape[1] - per_mem * full_rows
-        if missing:
-            blocks.append(jnp.zeros((missing, full_cols), jnp.float32))
-        stack = jnp.concatenate(blocks, axis=0).astype(jnp.bfloat16)
-        stack = product(stack, perm_cols[...]).astype(jnp.bfloat16)
-        field[group] = product(perm_rows[...], stack)
+            block = jnp.where(scaled[1] > 0.5, block, 0.0)
+            field[group, k] = interleaved(natural.at[k], block)
         return carry
 
     lax.fori_loop(0, mem_count, build, 0)
@@ -377,18 +344,21 @@
 
     def step_work(step, carry):
         group = group_at(step)
-        scaled[0] = extended(grads[group])
-        total = jnp.zeros((full_rows, full_cols), jnp.float32)
+        scaled[0] = extended(grads[group], 0)
+        total = jnp.zeros((full_rows, cols), jnp.float32)
         for k in range(per_mem):
-            here = slice(k * full_rows, (k + 1) * full_rows)
-            values = field[group, here] * scaled[0]
+            values = field[group, k] * scaled[0]
             values = one_pass(values, 5)
             values = one_pass(values, 5)
             values = one_pass(values, 1)
             values = one_pass(values, 1)
-            total = total + values * field[group, here]
-        total = product(parts_of(total), back_cols[...]).astype(jnp.bfloat16)
-        sums[0, group] = product(back_parts[...], total)
+            total = total + values[:, :cols] * field[group, k, :, :cols]
+        tiles = full_rows // SUB
+        for u, column in enumerate(columns_of(total)):
+            for t in range(tiles):
+                wide_sums[group, u, pl.ds(t, SUB, stride=tiles), :] = column[
+                    t * SUB : (t + 1) * SUB
+                ]
 
         @pl.when(step + 1 < mem_count)
         def _():
@@ -397,11 +367,12 @@
         return carry
 
     lax.fori_loop(0, mem_count, step_work, 0)
-    total = sums[0, 0]
+    total = wide_sums[0, :, :rows]
     for offset in range(1, mem_count):
         back(jnp.int32(offset)).wait_recv()
-        total = total + sums[1, offset]
-    out[0] = total * scale
+        total = total + sums[offset]
+    for u in range(cols // LANES):
+        out[0, :, u * LANES : (u + 1) * LANES] = total[u] * scale
 
     for offset in range(1, mem_count):
         across(jnp.int32(offset)).wait_send()
@@ -431,7 +402,7 @@
         out_specs=pl.BlockSpec(memory_space=pltpu.VMEM),
         scratch_shapes=[
             pltpu.VMEM((per_mem, mem_count, rows, cols), jnp.bfloat16),
-            pltpu.VMEM((mem_count, per_mem * full_rows, full_cols), jnp.float32),
+            pltpu.VMEM((mem_count, per_mem, full_rows, full_cols), jnp.float32),
             pltpu.VMEM((2, mem_count, packed, cols), jnp.bfloat16),
             pltpu.VMEM((2, mem_count, rows, LANES), jnp.bfloat16),
             pltpu.VMEM((2, mem_count, packed, cols + 2 * LANES), jnp.bfloat16),
@@ -440,12 +411,9 @@
             pltpu.VMEM((9, full_rows, full_cols), jnp.float32),
             pltpu.VMEM((2, full_rows, full_cols), jnp.float32),
             pltpu.VMEM((mem_count, rows + 2 * SUB, cols + 2 * LANES), jnp.float32),
-            pltpu.VMEM((2, mem_count, rows, cols), jnp.float32),
-            pltpu.VMEM((full_cols, full_cols), jnp.bfloat16),
-            pltpu.VMEM((per_mem * full_rows, -(-per_mem * full_rows // 16) * 16), jnp.bfloat16),
-            pltpu.VMEM((full_rows, 3 * full_rows + SUB), jnp.bfloat16),
-            pltpu.VMEM((full_cols, cols), jnp.bfloat16),
-            pltpu.VMEM((rows, 3 * full_rows + SUB), jnp.bfloat16),
+            pltpu.VMEM((mem_count, cols // LANES, rows, LANES), jnp.float32),
+            pltpu.VMEM((mem_count, cols // LANES, full_rows, LANES), jnp.float32),
+            pltpu.VMEM((max(5, per_mem), full_cols // LANES, full_rows, LANES), jnp.float32),
             pltpu.SemaphoreType.DMA((mem_count,)),
             pltpu.SemaphoreType.DMA((mem_count,)),
             pltpu.SemaphoreType.DMA((mem_count,)),

time: 23.6 us -> 24.1 us (1.021)
  Pallas kernels: 22.1 us -> 22.6 us
    pallas_call x1, Pallas kernels: 22.1 us -> 22.6 us  [body(): pl.pallas_call(functools.partial(kernel, sizes), out_shape=jax.ShapeDtype...]
where the time goes in v6:
time: 24.1 us; the launch traced here: 23.9 us
  Pallas kernels  22.6 us (94%)
  local copies, waits for them, and re-layouts  1.38 us (6%)
    pallas_call x1, Pallas kernels, body(): pl.pallas_call(functools.partial(kernel, sizes), out_shape=jax.ShapeDtype...  22.6 us
    unnamed x1, local copies, waits for them, and re-layouts  1.38 us

profile of v6, /device:TPU:0, one launch (start us, length us, event | category | flops | bytes accessed | tf_op | source)
XLA Modules:
  0.0 23.9 jit_solution(10630708611993341855)
XLA Ops:
  0.0 22.6 %shard_map.37 = f32[1,32,256]{2,1,0:T(8,128)} custom-call(bf16[5,4,32,256]{3,2,1,0:T(8,128)(2,1)} %pert.1, f32[1,32,256]{2,1,0:T(8,128)} %grad.1, f32[5,32,256]{2,1,0:T(8,128)} %coef.1), custom_call_target="tpu_custom_call" | custom-call | tf_op jit(solution)/shard_map/pallas_call | solution.py:398
  22.6 1.4 %copy.5 = f32[1,32,256]{2,1,0:T(8,128)} copy(f32[1,32,256]{2,1,0:T(8,128)} %shard_map.37) | data formatting | bytes 65536

commit v7 on v6

--- a/solution.py
+++ b/solution.py
@@ -346,13 +346,16 @@
         group = group_at(step)
         scaled[0] = extended(grads[group], 0)
         total = jnp.zeros((full_rows, cols), jnp.float32)
-        for k in range(per_mem):
+
+        def member(k, total):
             values = field[group, k] * scaled[0]
             values = one_pass(values, 5)
             values = one_pass(values, 5)
             values = one_pass(values, 1)
             values = one_pass(values, 1)
-            total = total + values[:, :cols] * field[group, k, :, :cols]
+            return total + values[:, :cols] * field[group, k, :, :cols]
+
+        total = lax.fori_loop(0, per_mem, member, total)
         tiles = full_rows // SUB
         for u, column in enumerate(columns_of(total)):
             for t in range(tiles):
@@ -423,7 +426,7 @@
             pltpu.SemaphoreType.DMA((3,)),
         ],
         compiler_params=pltpu.CompilerParams(
-            collective_id=0, has_side_effects=True, vmem_limit_bytes=60 * 1024 * 1024
+            collective_id=0, has_side_effects=True, vmem_limit_bytes=55192 * 1024
         ),
     )(perturbations, gradient, filter_coef)
 

time: 24.1 us -> 24.3 us (level)
  Pallas kernels: 22.6 us -> 23.6 us
  local copies, waits for them, and re-layouts: 1.38 us -> 0.62 us
    pallas_call x1, Pallas kernels: 22.6 us -> 23.6 us  [body(): pl.pallas_call(functools.partial(kernel, sizes), out_shape=jax.ShapeDtype...]
    unnamed x1, local copies, waits for them, and re-layouts: 1.38 us -> 0.62 us
where the time goes in v7:
time: 24.3 us; the launch traced here: 24.2 us
  Pallas kernels  23.6 us (97%)
  local copies, waits for them, and re-layouts  0.62 us (3%)
    pallas_call x1, Pallas kernels, body(): pl.pallas_call(functools.partial(kernel, sizes), out_shape=jax.ShapeDtype...  23.6 us
    unnamed x1, local copies, waits for them, and re-layouts  0.62 us

profile of v7, /device:TPU:0, one launch (start us, length us, event | category | flops | bytes accessed | tf_op | source)
XLA Modules:
  0.0 24.2 jit_solution(10795991939822533381)
XLA Ops:
  0.0 23.6 %shard_map.37 = f32[1,32,256]{2,1,0:T(8,128)S(1)} custom-call(bf16[5,4,32,256]{3,2,1,0:T(8,128)(2,1)} %pert.1, f32[1,32,256]{2,1,0:T(8,128)} %grad.1, f32[5,32,256]{2,1,0:T(8,128)} %coef.1), custom_call_target="tpu_custom_call" | custom-call | tf_op jit(solution)/shard_map/pallas_call | solution.py:401
  23.6 0.6 %copy.5 = f32[1,32,256]{2,1,0:T(8,128)} copy(f32[1,32,256]{2,1,0:T(8,128)S(1)} %shard_map.37) | data formatting | bytes 65536

commit v8 on v6

--- a/solution.py
+++ b/solution.py
@@ -14,14 +14,23 @@
 
 
 def shifted(values, offset, axis):
+    unit = (SUB, LANES)[axis]
     size = values.shape[axis]
-    if axis == 1:
-        return pltpu.roll(values, (-offset) % size, 1)
     if offset < 0:
-        edge = pltpu.roll(values[size - SUB :], 1, 0)
-        return jnp.concatenate([edge, values[: size - SUB]], axis=0)
-    edge = pltpu.roll(values[:SUB], SUB - 1, 0)
-    return jnp.concatenate([values[SUB:], edge], axis=0)
+        edge = pltpu.roll(lax.slice_in_dim(values, size - unit, size, axis=axis), 1, axis)
+        return jnp.concatenate([edge, lax.slice_in_dim(values, 0, size - unit, axis=axis)], axis=axis)
+    edge = pltpu.roll(lax.slice_in_dim(values, 0, unit, axis=axis), unit - 1, axis)
+    return jnp.concatenate([lax.slice_in_dim(values, unit, size, axis=axis), edge], axis=axis)
+
+
+def moved(values, matrix):
+    high = values.astype(jnp.bfloat16).astype(jnp.float32)
+    rest = values - high
+    middle = rest.astype(jnp.bfloat16).astype(jnp.float32)
+    parts = jnp.concatenate([high, middle, rest - middle], axis=0).astype(jnp.bfloat16)
+    result = jnp.dot(parts, matrix, preferred_element_type=jnp.float32)
+    size = values.shape[0]
+    return result[:size] + result[size : 2 * size] + result[2 * size :]
 
 
 def place_of(index, unit, size):
@@ -72,10 +81,12 @@
     ext,
     stencils,
     scaled,
+    level_grads,
     grads,
     sums,
-    wide_sums,
     natural,
+    perm_cols,
+    back_cols,
     z_send,
     z_recv,
     sum_send,
@@ -154,7 +165,16 @@
     )
     inside = inside_of(row_index, col_index)
     scaled[1] = inside.astype(jnp.float32)
-    inside_here = inside_of(place_of(row_index, SUB, full_rows), col_index)
+    inside_here = inside_of(
+        place_of(row_index, SUB, full_rows), place_of(col_index, LANES, full_cols)
+    )
+
+    place = place_of(lax.broadcasted_iota(jnp.int32, (1, full_cols), 1), LANES, full_cols)
+    source = lax.broadcasted_iota(jnp.int32, perm_cols.shape, 0)
+    perm_cols[...] = jnp.where(source == place, 1.0, 0.0).astype(jnp.bfloat16)
+    place = place_of(lax.broadcasted_iota(jnp.int32, (full_cols, 1), 0), LANES, full_cols)
+    target = lax.broadcasted_iota(jnp.int32, back_cols.shape, 1)
+    back_cols[...] = jnp.where(target == place, 1.0, 0.0).astype(jnp.bfloat16)
     low_row_full = lax.broadcasted_iota(jnp.int32, (SUB, full_cols), 0) < HALO
 
     blocks = [
@@ -175,8 +195,8 @@
 
     def back(offset):
         return pltpu.make_async_remote_copy(
-            src_ref=wide_sums.at[offset, :, pl.ds(0, rows)],
-            dst_ref=sums.at[offset],
+            src_ref=sums.at[0, offset],
+            dst_ref=sums.at[1, offset],
             send_sem=sum_send.at[offset],
             recv_sem=sum_recv.at[offset],
             device_id=(peer(offset), lat, lon),
@@ -290,14 +310,21 @@
     own_coef.wait()
     for_sources(lambda number, direction: coef_copy(number, direction).wait_recv())
 
-    def extended(block, slot):
-        wide = folded(block, cols)
-        wide = circular(
-            wide[SUB : SUB + rows], wide[:SUB], wide[SUB + rows :], low_row_full
-        )
-        return interleaved(natural.at[slot], jnp.where(scaled[1] > 0.5, wide, 0.0))
-
-    c0, cn, cs, cw, ce = (extended(ext[index], index) for index in range(5))
+    def extended(blocks):
+        stack = []
+        for block in blocks:
+            wide = folded(block, cols)
+            wide = circular(
+                wide[SUB : SUB + rows], wide[:SUB], wide[SUB + rows :], low_row_full
+            )
+            stack.append(jnp.where(scaled[1] > 0.5, wide, 0.0))
+        stack = moved(jnp.concatenate(stack, axis=0), perm_cols[...])
+        return [
+            interleaved(natural.at[index], stack[index * full_rows : (index + 1) * full_rows])
+            for index in range(len(blocks))
+        ]
+
+    c0, cn, cs, cw, ce = extended([ext[index] for index in range(5)])
     for index, value in enumerate((c0, cn, cs, cw, ce)):
         stencils[index] = value
     for index, value in enumerate(
@@ -322,6 +349,7 @@
         north = folded(recv_rows[1, group].astype(jnp.float32), cols)
         from_east = recv_cols[0, group].astype(jnp.float32)
         from_west = recv_cols[1, group].astype(jnp.float32)
+        blocks = []
         for k in range(per_mem):
             block = centre[k, peer(group)].astype(jnp.float32)
             tile = slice((k // 2) * SUB, (k // 2 + 1) * SUB)
@@ -335,30 +363,38 @@
             block = circular(
                 jnp.concatenate([block, side], axis=1), north_rows, south_rows, low_row_full
             )
-            block = jnp.where(scaled[1] > 0.5, block, 0.0)
+            blocks.append(jnp.where(scaled[1] > 0.5, block, 0.0))
+        stack = jnp.concatenate(blocks, axis=0).astype(jnp.bfloat16)
+        stack = jnp.dot(stack, perm_cols[...], preferred_element_type=jnp.float32)
+        for k in range(per_mem):
+            block = stack[k * full_rows : (k + 1) * full_rows]
             field[group, k] = interleaved(natural.at[k], block)
         return carry
 
     lax.fori_loop(0, mem_count, build, 0)
     for_sources(lambda number, direction: grad_copy(number, direction).wait_recv())
 
+    for index, value in enumerate(extended([grads[index] for index in range(mem_count)])):
+        level_grads[index] = value
+
     def step_work(step, carry):
         group = group_at(step)
-        scaled[0] = extended(grads[group], 0)
-        total = jnp.zeros((full_rows, cols), jnp.float32)
+        total = jnp.zeros((full_rows, full_cols), jnp.float32)
         for k in range(per_mem):
-            values = field[group, k] * scaled[0]
+            values = field[group, k] * level_grads[group]
             values = one_pass(values, 5)
             values = one_pass(values, 5)
             values = one_pass(values, 1)
             values = one_pass(values, 1)
-            total = total + values[:, :cols] * field[group, k, :, :cols]
+            total = total + values * field[group, k]
         tiles = full_rows // SUB
         for u, column in enumerate(columns_of(total)):
             for t in range(tiles):
-                wide_sums[group, u, pl.ds(t, SUB, stride=tiles), :] = column[
-                    t * SUB : (t + 1) * SUB
-                ]
+                natural[0, u, pl.ds(t, SUB, stride=tiles), :] = column[t * SUB : (t + 1) * SUB]
+        total = jnp.concatenate(
+            [natural[0, u, :rows, :] for u in range(full_cols // LANES)], axis=1
+        )
+        sums[0, group] = moved(total, back_cols[...])
 
         @pl.when(step + 1 < mem_count)
         def _():
@@ -367,12 +403,11 @@
         return carry
 
     lax.fori_loop(0, mem_count, step_work, 0)
-    total = wide_sums[0, :, :rows]
+    total = sums[0, 0]
     for offset in range(1, mem_count):
         back(jnp.int32(offset)).wait_recv()
-        total = total + sums[offset]
-    for u in range(cols // LANES):
-        out[0, :, u * LANES : (u + 1) * LANES] = total[u] * scale
+        total = total + sums[1, offset]
+    out[0] = total * scale
 
     for offset in range(1, mem_count):
         across(jnp.int32(offset)).wait_send()
@@ -410,10 +445,12 @@
             pltpu.VMEM((5, rows + 2 * SUB, cols + 2 * LANES), jnp.float32),
             pltpu.VMEM((9, full_rows, full_cols), jnp.float32),
             pltpu.VMEM((2, full_rows, full_cols), jnp.float32),
+            pltpu.VMEM((mem_count, full_rows, full_cols), jnp.float32),
             pltpu.VMEM((mem_count, rows + 2 * SUB, cols + 2 * LANES), jnp.float32),
-            pltpu.VMEM((mem_count, cols // LANES, rows, LANES), jnp.float32),
-            pltpu.VMEM((mem_count, cols // LANES, full_rows, LANES), jnp.float32),
-            pltpu.VMEM((max(5, per_mem), full_cols // LANES, full_rows, LANES), jnp.float32),
+            pltpu.VMEM((2, mem_count, rows, cols), jnp.float32),
+            pltpu.VMEM((max(5, per_mem, mem_count), full_cols // LANES, full_rows, LANES), jnp.float32),
+            pltpu.VMEM((full_cols, full_cols), jnp.bfloat16),
+            pltpu.VMEM((full_cols, cols), jnp.bfloat16),
             pltpu.SemaphoreType.DMA((mem_count,)),
             pltpu.SemaphoreType.DMA((mem_count,)),
             pltpu.SemaphoreType.DMA((mem_count,)),
@@ -423,7 +460,7 @@
             pltpu.SemaphoreType.DMA((3,)),
         ],
         compiler_params=pltpu.CompilerParams(
-            collective_id=0, has_side_effects=True, vmem_limit_bytes=60 * 1024 * 1024
+            collective_id=0, has_side_effects=True, vmem_limit_bytes=55192 * 1024
         ),
     )(perturbations, gradient, filter_coef)
 

time: 24.1 us -> 21.1 us (0.88)
  Pallas kernels: 22.6 us -> 20.3 us
  local copies, waits for them, and re-layouts: 1.38 us -> 0.62 us
    pallas_call x1, Pallas kernels: 22.6 us -> 20.3 us  [body(): pl.pallas_call(functools.partial(kernel, sizes), out_shape=jax.ShapeDtype...]
    unnamed x1, local copies, waits for them, and re-layouts: 1.38 us -> 0.62 us
where the time goes in v8:
time: 21.1 us; the launch traced here: 21 us
  Pallas kernels  20.3 us (96%)
  local copies, waits for them, and re-layouts  0.62 us (3%)
    pallas_call x1, Pallas kernels, body(): pl.pallas_call(functools.partial(kernel, sizes), out_shape=jax.ShapeDtype...  20.3 us
    unnamed x1, local copies, waits for them, and re-layouts  0.62 us

profile of v8, /device:TPU:0, one launch (start us, length us, event | category | flops | bytes accessed | tf_op | source)
XLA Modules:
  0.0 21.0 jit_solution(9437749146872799164)
XLA Ops:
  0.0 20.3 %shard_map.37 = f32[1,32,256]{2,1,0:T(8,128)S(1)} custom-call(bf16[5,4,32,256]{3,2,1,0:T(8,128)(2,1)} %pert.1, f32[1,32,256]{2,1,0:T(8,128)} %grad.1, f32[5,32,256]{2,1,0:T(8,128)} %coef.1), custom_call_target="tpu_custom_call" | custom-call | tf_op jit(solution)/shard_map/pallas_call | solution.py:433
  20.3 0.6 %copy.5 = f32[1,32,256]{2,1,0:T(8,128)} copy(f32[1,32,256]{2,1,0:T(8,128)S(1)} %shard_map.37) | data formatting | bytes 65536

commit v9 on v8

--- a/solution.py
+++ b/solution.py
@@ -144,39 +144,6 @@
     own_grad.start()
     own_coef.start()
 
-    full_rows, full_cols = rows + 2 * HALO, cols + LANES
-
-    def inside_of(row_index, col_index):
-        row_index = jnp.where(row_index < rows + HALO, row_index, row_index - full_rows)
-        col_index = jnp.where(col_index < cols + LANES // 2, col_index, col_index - full_cols)
-        near = (col_index >= -HALO) & (col_index < cols + HALO)
-        row_index = row_index + lat * rows
-        col_index = col_index + lon * cols
-        return (
-            near
-            & (row_index >= 0)
-            & (row_index < rows * lat_count)
-            & (col_index >= 0)
-            & (col_index < cols * lon_count)
-        )
-
-    row_index, col_index = (
-        lax.broadcasted_iota(jnp.int32, (full_rows, full_cols), axis) for axis in range(2)
-    )
-    inside = inside_of(row_index, col_index)
-    scaled[1] = inside.astype(jnp.float32)
-    inside_here = inside_of(
-        place_of(row_index, SUB, full_rows), place_of(col_index, LANES, full_cols)
-    )
-
-    place = place_of(lax.broadcasted_iota(jnp.int32, (1, full_cols), 1), LANES, full_cols)
-    source = lax.broadcasted_iota(jnp.int32, perm_cols.shape, 0)
-    perm_cols[...] = jnp.where(source == place, 1.0, 0.0).astype(jnp.bfloat16)
-    place = place_of(lax.broadcasted_iota(jnp.int32, (full_cols, 1), 0), LANES, full_cols)
-    target = lax.broadcasted_iota(jnp.int32, back_cols.shape, 1)
-    back_cols[...] = jnp.where(target == place, 1.0, 0.0).astype(jnp.bfloat16)
-    low_row_full = lax.broadcasted_iota(jnp.int32, (SUB, full_cols), 0) < HALO
-
     blocks = [
         1 + jnp.where(here > 0, 1, 0) + jnp.where(here < count - 1, 1, 0)
         for here, count in ((lat, lat_count), (lon, lon_count))
@@ -273,6 +240,39 @@
                 action(number, direction)
 
     for_targets(lambda number, direction: coef_copy(number, direction).start())
+
+    full_rows, full_cols = rows + 2 * HALO, cols + LANES
+
+    def inside_of(row_index, col_index):
+        row_index = jnp.where(row_index < rows + HALO, row_index, row_index - full_rows)
+        col_index = jnp.where(col_index < cols + LANES // 2, col_index, col_index - full_cols)
+        near = (col_index >= -HALO) & (col_index < cols + HALO)
+        row_index = row_index + lat * rows
+        col_index = col_index + lon * cols
+        return (
+            near
+            & (row_index >= 0)
+            & (row_index < rows * lat_count)
+            & (col_index >= 0)
+            & (col_index < cols * lon_count)
+        )
+
+    row_index, col_index = (
+        lax.broadcasted_iota(jnp.int32, (full_rows, full_cols), axis) for axis in range(2)
+    )
+    inside = inside_of(row_index, col_index)
+    scaled[1] = inside.astype(jnp.float32)
+    inside_here = inside_of(
+        place_of(row_index, SUB, full_rows), place_of(col_index, LANES, full_cols)
+    )
+
+    place = place_of(lax.broadcasted_iota(jnp.int32, (1, full_cols), 1), LANES, full_cols)
+    source = lax.broadcasted_iota(jnp.int32, perm_cols.shape, 0)
+    perm_cols[...] = jnp.where(source == place, 1.0, 0.0).astype(jnp.bfloat16)
+    place = place_of(lax.broadcasted_iota(jnp.int32, (full_cols, 1), 0), LANES, full_cols)
+    target = lax.broadcasted_iota(jnp.int32, back_cols.shape, 1)
+    back_cols[...] = jnp.where(target == place, 1.0, 0.0).astype(jnp.bfloat16)
+    low_row_full = lax.broadcasted_iota(jnp.int32, (SUB, full_cols), 0) < HALO
 
     low_row = lax.broadcasted_iota(jnp.int32, (SUB, cols), 0) < HALO
     lane = lax.broadcasted_iota(jnp.int32, (rows, LANES), 1)
@@ -338,10 +338,6 @@
         total = total + stencils[first + 2] * shifted(values, -1, 1)
         return total + stencils[first + 3] * shifted(values, 1, 1)
 
-    own_grad.wait()
-    for offset in range(1, mem_count):
-        across(jnp.int32(offset)).wait_recv()
-    for_targets(lambda number, direction: grad_copy(number, direction).start())
     for_sources(lambda number, direction: pert_copy(number, direction).wait_recv())
 
     def build(group, carry):
@@ -371,7 +367,13 @@
             field[group, k] = interleaved(natural.at[k], block)
         return carry
 
-    lax.fori_loop(0, mem_count, build, 0)
+    early = mem_count // 2
+    lax.fori_loop(0, early, build, 0)
+    own_grad.wait()
+    for offset in range(1, mem_count):
+        across(jnp.int32(offset)).wait_recv()
+    for_targets(lambda number, direction: grad_copy(number, direction).start())
+    lax.fori_loop(early, mem_count, build, 0)
     for_sources(lambda number, direction: grad_copy(number, direction).wait_recv())
 
     for index, value in enumerate(extended([grads[index] for index in range(mem_count)])):

time: 21.1 us -> 22.7 us (1.076)
  Pallas kernels: 20.3 us -> 21.9 us
    pallas_call x1, Pallas kernels: 20.3 us -> 21.9 us  [body(): pl.pallas_call(functools.partial(kernel, sizes), out_shape=jax.ShapeDtype...]
where the time goes in v9:
time: 22.7 us; the launch traced here: 22.5 us
  Pallas kernels  21.9 us (96%)
  local copies, waits for them, and re-layouts  0.62 us (3%)
    pallas_call x1, Pallas kernels, body(): pl.pallas_call(functools.partial(kernel, sizes), out_shape=jax.ShapeDtype...  21.9 us
    unnamed x1, local copies, waits for them, and re-layouts  0.62 us

profile of v9, /device:TPU:0, one launch (start us, length us, event | category | flops | bytes accessed | tf_op | source)
XLA Modules:
  0.0 22.5 jit_solution(3964743154597311386)
XLA Ops:
  0.0 21.9 %shard_map.37 = f32[1,32,256]{2,1,0:T(8,128)S(1)} custom-call(bf16[5,4,32,256]{3,2,1,0:T(8,128)(2,1)} %pert.1, f32[1,32,256]{2,1,0:T(8,128)} %grad.1, f32[5,32,256]{2,1,0:T(8,128)} %coef.1), custom_call_target="tpu_custom_call" | custom-call | tf_op jit(solution)/shard_map/pallas_call | solution.py:435
  21.9 0.6 %copy.5 = f32[1,32,256]{2,1,0:T(8,128)} copy(f32[1,32,256]{2,1,0:T(8,128)S(1)} %shard_map.37) | data formatting | bytes 65536

commit v10 on v8

--- a/solution.py
+++ b/solution.py
@@ -307,6 +307,10 @@
     own_pert.wait()
     lax.fori_loop(0, mem_count, pack, 0)
     for_targets(lambda number, direction: pert_copy(number, direction).start())
+    own_grad.wait()
+    for offset in range(1, mem_count):
+        across(jnp.int32(offset)).wait_recv()
+    for_targets(lambda number, direction: grad_copy(number, direction).start())
     own_coef.wait()
     for_sources(lambda number, direction: coef_copy(number, direction).wait_recv())
 
@@ -338,10 +342,6 @@
         total = total + stencils[first + 2] * shifted(values, -1, 1)
         return total + stencils[first + 3] * shifted(values, 1, 1)
 
-    own_grad.wait()
-    for offset in range(1, mem_count):
-        across(jnp.int32(offset)).wait_recv()
-    for_targets(lambda number, direction: grad_copy(number, direction).start())
     for_sources(lambda number, direction: pert_copy(number, direction).wait_recv())
 
     def build(group, carry):

time: 21.1 us -> 21.1 us (level)
  no operation moved by 1% of the time
where the time goes in v10:
time: 21.1 us; the launch traced here: 21 us
  Pallas kernels  20.3 us (96%)
  local copies, waits for them, and re-layouts  0.62 us (3%)
    pallas_call x1, Pallas kernels, body(): pl.pallas_call(functools.partial(kernel, sizes), out_shape=jax.ShapeDtype...  20.3 us
    unnamed x1, local copies, waits for them, and re-layouts  0.62 us

profile of v10, /device:TPU:0, one launch (start us, length us, event | category | flops | bytes accessed | tf_op | source)
XLA Modules:
  0.0 21.0 jit_solution(4674990259007187837)
XLA Ops:
  0.0 20.3 %shard_map.37 = f32[1,32,256]{2,1,0:T(8,128)S(1)} custom-call(bf16[5,4,32,256]{3,2,1,0:T(8,128)(2,1)} %pert.1, f32[1,32,256]{2,1,0:T(8,128)} %grad.1, f32[5,32,256]{2,1,0:T(8,128)} %coef.1), custom_call_target="tpu_custom_call" | custom-call | tf_op jit(solution)/shard_map/pallas_call | solution.py:433
  20.3 0.6 %copy.5 = f32[1,32,256]{2,1,0:T(8,128)} copy(f32[1,32,256]{2,1,0:T(8,128)S(1)} %shard_map.37) | data formatting | bytes 65536
